TPU v7x, 32 devices: a whole 2x2x4 slice. The times are simulated.
32 devices in a mesh: dp: 16 (over z, x, core), mp: 2 (over y).
Axes of the slice: x: 2, y: 2, z: 4, core: 2. Of those that a mesh axis runs over, the one named last changes fastest.
Arguments:
- tokens: bfloat16 [32768, 768], P('dp'), may hold values from -6 to 6
- lengths: int32 [128], P('dp'), may hold values from 64 to 256, as said below
- queries: bfloat16 [192, 768], P('dp'), may hold values from -0.4375 to 0.4375
- positives: int32 [192], replicated, may hold values from 0 to 127
- w_qkv: bfloat16 [3, 768, 768], P(None, None, 'mp'), may hold values from -0.21875 to 0.21875
- b_qv: bfloat16 [2, 768], P(None, 'mp'), may hold values from -1.796875 to 1.796875
- w_out: bfloat16 [768, 768], P('mp'), may hold values from -1.75 to 1.75
- b_out: bfloat16 [768], replicated, may hold values from -1.796875 to 1.796875
- gain_one: bfloat16 [768], replicated, may hold values from 0.5 to 1.5
- shift_one: bfloat16 [768], replicated, may hold values from -1.796875 to 1.796875
- w_in: bfloat16 [768, 3072], P(None, 'mp'), may hold values from -0.21875 to 0.21875
- b_in: bfloat16 [3072], P('mp'), may hold values from -3 to 3
- w_back: bfloat16 [3072, 768], P('mp'), may hold values from -0.109375 to 0.109375
- b_back: bfloat16 [768], replicated, may hold values from -1.796875 to 1.796875
- gain_two: bfloat16 [768], replicated, may hold values from 0.5 to 1.5
Outputs:
- activations: bfloat16 [32768, 768], P('dp', 'mp')
- query_loss: float32 [192], P('dp')
- input_grad: float32 [32768, 768], P('dp', 'mp')
- query_grad: float32 [192, 768], P('dp')
- grad_qkv: float32 [3, 768, 768], P(None, 'dp', 'mp')
- grad_bias_qv: float32 [2, 768], P(None, ('mp', 'dp'))
- grad_out: float32 [768, 768], P('mp', 'dp')
- grad_bias_out: float32 [768], P('dp')
- grad_gain_one: float32 [768], P('dp')
- grad_shift_one: float32 [768], P('dp')
- grad_in: float32 [768, 3072], P('dp', 'mp')
- grad_bias_in: float32 [3072], P(('mp', 'dp'))
- grad_back: float32 [3072, 768], P('mp', 'dp')
- grad_bias_back: float32 [768], P('dp')
- grad_gain_two: float32 [768], P('dp')
Inputs may be any that keep to these rules, and one draw needn't show every extreme that they name: `lengths`: each passage has 64 or 256 tokens, both occur in every draw; the rest of its slot is padding.
All inputs are finite; a program needn't handle non-finite values.
Results may differ from a plain program's by a relative error of at most 0.029.
Values may be sent and summed in bfloat16 or wider, within the bound.
A program may use at most 192 MiB of HBM per device.

v0:
```python
import math

import jax
import jax.numpy as jnp
from jax import lax
from jax.sharding import PartitionSpec as P

HEAD = 64


epsilon = 1e-05
masked = -1e30


def layer_norm(rows, gain, shift):
    center = jnp.mean(rows, axis=-1, keepdims=True)
    spread = rows - center
    second = jnp.mean(spread * spread, axis=-1, keepdims=True)
    return spread * lax.rsqrt(second + epsilon) * gain + shift


def scaled_norm(rows, gain):
    center = jnp.mean(rows, axis=-1, keepdims=True)
    spread = rows - center
    second = jnp.mean(spread * spread, axis=-1, keepdims=True)
    return spread * lax.rsqrt(second + epsilon) * gain


def gelu_exact(values):
    return jax.nn.gelu(values, approximate=False)


def first_rows(values, count):
    return values.reshape((count, values.shape[0] // count) + values.shape[1:])[:, 0]


def per_device(
    tokens,
    lengths,
    queries,
    positives,
    w_qkv,
    b_qv,
    w_out,
    b_out,
    gain_one,
    shift_one,
    w_in,
    b_in,
    w_back,
    b_back,
    gain_two,
):
    rows, width = tokens.shape
    count = lengths.shape[0]
    slot = rows // count
    local = w_qkv.shape[2]
    heads_here = local // HEAD
    scale = 1.0 / math.sqrt(HEAD)
    projected = jnp.einsum("rd,jdc->jrc", tokens, w_qkv, preferred_element_type=jnp.float32)
    bias_qv = b_qv.astype(jnp.float32)
    query = (projected[0] + bias_qv[0]).astype(jnp.bfloat16)
    keyed = projected[1].astype(jnp.bfloat16)
    value = (projected[2] + bias_qv[1]).astype(jnp.bfloat16)
    block = min(count, max(1, 512 // slot))
    blocks = count // block
    valid = lax.broadcasted_iota(jnp.int32, (count, slot), 1) < lengths[:, None]
    split_shape = (blocks, block, slot, heads_here, HEAD)

    def attend(inputs):
        query_part, keyed_part, value_part, valid_part = inputs
        scores = (
            jnp.einsum(
                "pqhd,pkhd->phqk", query_part, keyed_part, preferred_element_type=jnp.float32
            )
            * scale
        )
        scores = jnp.where(valid_part[:, None, None, :], scores, masked)
        top = jnp.max(scores, axis=-1, keepdims=True)
        raised = jnp.exp(scores - top)
        total = jnp.sum(raised, axis=-1, keepdims=True)
        chance_low = (raised / total).astype(jnp.bfloat16)
        mixed = jnp.einsum(
            "phqk,pkhd->pqhd", chance_low, value_part, preferred_element_type=jnp.float32
        )
        return (mixed.astype(jnp.bfloat16), (top + jnp.log(total))[:, :, 0, 0])

    context, log_total = lax.map(
        attend,
        (
            query.reshape(split_shape),
            keyed.reshape(split_shape),
            value.reshape(split_shape),
            valid.reshape(blocks, block, slot),
        ),
    )
    context = context.reshape(rows, local)
    log_total = log_total.reshape(count, heads_here)
    partial_attn = jnp.dot(context, w_out, preferred_element_type=jnp.float32).astype(jnp.bfloat16)
    attended = lax.psum(partial_attn, "mp").astype(jnp.float32) + b_out.astype(jnp.float32)
    resid_one = tokens.astype(jnp.float32) + attended
    gain_one_w = gain_one.astype(jnp.float32)
    shift_one_w = shift_one.astype(jnp.float32)
    gain_two_w = gain_two.astype(jnp.float32)
    norm_one = layer_norm(resid_one, gain_one_w, shift_one_w)
    norm_low = norm_one.astype(jnp.bfloat16)
    inner = jnp.dot(norm_low, w_in, preferred_element_type=jnp.float32) + b_in.astype(jnp.float32)
    active = gelu_exact(inner).astype(jnp.bfloat16)
    partial_ffn = jnp.dot(active, w_back, preferred_element_type=jnp.float32).astype(jnp.bfloat16)
    resid_two = (
        norm_one + lax.psum(partial_ffn, "mp").astype(jnp.float32) + b_back.astype(jnp.float32)
    )
    output = scaled_norm(resid_two, gain_two_w)
    column = lax.axis_index("mp") * local
    activations = lax.dynamic_slice_in_dim(output, column, local, 1).astype(jnp.bfloat16)
    cls_low = first_rows(output, count).astype(jnp.bfloat16)
    query_rows = queries.shape[0]
    members = lax.axis_size("dp")
    query_total = query_rows * members
    own_query = lax.axis_index("dp") * query_rows
    gathered = lax.all_gather(cls_low, "dp", axis=0, tiled=True)
    similar = jnp.einsum("qd,pd->qp", queries, gathered, preferred_element_type=jnp.float32)
    mine = lax.dynamic_slice_in_dim(positives, own_query, query_rows)
    target = lax.broadcasted_iota(jnp.int32, similar.shape, 1) == mine[:, None]
    top = jnp.max(similar, axis=1, keepdims=True)
    log_sum = top[:, 0] + jnp.log(jnp.sum(jnp.exp(similar - top), axis=1))
    picked = jnp.sum(jnp.where(target, similar, 0.0), axis=1)
    query_loss = log_sum - picked
    slopes = (jnp.exp(similar - log_sum[:, None]) - target.astype(jnp.float32)) / query_total
    query_grad = jnp.dot(slopes, gathered.astype(jnp.float32), precision=lax.Precision.HIGHEST)
    queries_wide = queries.astype(jnp.float32)
    cls_grad = lax.psum_scatter(
        jnp.einsum("qp,qd->pd", slopes, queries_wide, precision=lax.Precision.HIGHEST),
        "dp",
        scatter_dimension=0,
        tiled=True,
    )
    _, norm_two_pull = jax.vjp(scaled_norm, first_rows(resid_two, count), gain_two_w)
    d_resid_two, grad_gain_two = norm_two_pull(cls_grad)
    grad_bias_back = jnp.sum(d_resid_two, axis=0)
    ffn_low = d_resid_two.astype(jnp.bfloat16)
    grad_back = jnp.einsum(
        "pf,pd->fd", first_rows(active, count), ffn_low, preferred_element_type=jnp.float32
    )
    d_active = jnp.einsum("pd,fd->pf", ffn_low, w_back, preferred_element_type=jnp.float32)
    _, gelu_pull = jax.vjp(gelu_exact, first_rows(inner, count))
    d_inner = gelu_pull(d_active)[0]
    grad_bias_in = jnp.sum(d_inner, axis=0)
    inner_low = d_inner.astype(jnp.bfloat16)
    grad_in = jnp.einsum(
        "pd,pf->df", first_rows(norm_low, count), inner_low, preferred_element_type=jnp.float32
    )
    back_norm = jnp.einsum("pf,df->pd", inner_low, w_in, preferred_element_type=jnp.float32)
    d_norm_one = d_resid_two + lax.psum(back_norm, "mp")
    _, norm_one_pull = jax.vjp(layer_norm, first_rows(resid_one, count), gain_one_w, shift_one_w)
    d_resid_one, grad_gain_one, grad_shift_one = norm_one_pull(d_norm_one)
    grad_bias_out = jnp.sum(d_resid_one, axis=0)
    attn_low = d_resid_one.astype(jnp.bfloat16)
    grad_out = jnp.einsum(
        "pc,pd->cd", first_rows(context, count), attn_low, preferred_element_type=jnp.float32
    )
    d_context = jnp.einsum("pd,cd->pc", attn_low, w_out, preferred_element_type=jnp.float32).astype(
        jnp.bfloat16
    )
    d_context = d_context.reshape(count, heads_here, HEAD)
    query_cls = first_rows(query, count).reshape(count, heads_here, HEAD)
    keyed_heads = keyed.reshape(count, slot, heads_here, HEAD)
    value_heads = value.reshape(count, slot, heads_here, HEAD)
    scores_cls = (
        jnp.einsum("phd,pkhd->phk", query_cls, keyed_heads, preferred_element_type=jnp.float32)
        * scale
    )
    scores_cls = jnp.where(valid[:, None, :], scores_cls, masked)
    chance = jnp.exp(scores_cls - log_total[:, :, None])
    d_chance = jnp.einsum(
        "phd,pkhd->phk", d_context, value_heads, preferred_element_type=jnp.float32
    )
    d_value = jnp.einsum(
        "phk,phd->pkhd", chance.astype(jnp.bfloat16), d_context, preferred_element_type=jnp.float32
    )
    d_scores = chance * (d_chance - jnp.sum(chance * d_chance, axis=-1, keepdims=True))
    scores_low = d_scores.astype(jnp.bfloat16)
    d_query = (
        jnp.einsum("phk,pkhd->phd", scores_low, keyed_heads, preferred_element_type=jnp.float32)
        * scale
    )
    d_keyed = (
        jnp.einsum("phk,phd->pkhd", scores_low, query_cls, preferred_element_type=jnp.float32)
        * scale
    )
    d_query = d_query.reshape(count, local)
    d_value = d_value.reshape(rows, local)
    query_low = d_query.astype(jnp.bfloat16)
    keyed_value_low = jnp.stack(
        [d_keyed.reshape(rows, local).astype(jnp.bfloat16), d_value.astype(jnp.bfloat16)]
    )
    grad_bias_qv = jnp.stack([jnp.sum(d_query, axis=0), jnp.sum(d_value, axis=0)])
    grad_query_w = jnp.einsum(
        "pd,pc->dc", first_rows(tokens, count), query_low, preferred_element_type=jnp.float32
    )
    grad_kv = jnp.einsum("rd,jrc->jdc", tokens, keyed_value_low, preferred_element_type=jnp.float32)
    grad_qkv = jnp.concatenate([grad_query_w[None], grad_kv], axis=0)
    own_half = lax.dynamic_slice_in_dim(d_resid_one, column, local, 1)
    back_kv = jnp.einsum(
        "jrc,jdc->rd", keyed_value_low, w_qkv[1:], preferred_element_type=jnp.float32
    )
    back_query = jnp.einsum("pc,dc->pd", query_low, w_qkv[0], preferred_element_type=jnp.float32)
    back_all = back_kv.reshape(count, slot, width).at[:, 0].add(back_query).reshape(rows, width)
    input_grad = lax.psum_scatter(
        back_all.astype(jnp.bfloat16), "mp", scatter_dimension=1, tiled=True
    ).astype(jnp.float32)
    input_grad = input_grad.reshape(count, slot, local).at[:, 0].add(own_half).reshape(rows, local)
    summed = (
        lax.psum_scatter(grad_qkv, "dp", scatter_dimension=1, tiled=True),
        lax.psum_scatter(grad_bias_qv, "dp", scatter_dimension=1, tiled=True),
        lax.psum_scatter(grad_out, "dp", scatter_dimension=1, tiled=True),
        lax.psum_scatter(grad_bias_out, "dp", scatter_dimension=0, tiled=True),
        lax.psum_scatter(grad_gain_one, "dp", scatter_dimension=0, tiled=True),
        lax.psum_scatter(grad_shift_one, "dp", scatter_dimension=0, tiled=True),
        lax.psum_scatter(grad_in, "dp", scatter_dimension=0, tiled=True),
        lax.psum_scatter(grad_bias_in, "dp", scatter_dimension=0, tiled=True),
        lax.psum_scatter(grad_back, "dp", scatter_dimension=1, tiled=True),
        lax.psum_scatter(grad_bias_back, "dp", scatter_dimension=0, tiled=True),
        lax.psum_scatter(grad_gain_two, "dp", scatter_dimension=0, tiled=True),
    )
    return (
        activations,
        query_loss,
        input_grad,
        query_grad,
        summed[0],
        summed[1],
        summed[2],
        summed[3],
        summed[4],
        summed[5],
        summed[6],
        summed[7],
        summed[8],
        summed[9],
        summed[10],
    )


def solution(mesh):
    in_specs = (
        P("dp", None),
        P("dp"),
        P("dp", None),
        P(),
        P(None, None, "mp"),
        P(None, "mp"),
        P("mp", None),
        P(),
        P(),
        P(),
        P(None, "mp"),
        P("mp"),
        P("mp", None),
        P(),
        P(),
    )
    out_specs = (
        P("dp", "mp"),
        P("dp"),
        P("dp", "mp"),
        P("dp", None),
        P(None, "dp", "mp"),
        P(None, ("mp", "dp")),
        P("mp", "dp"),
        P("dp"),
        P("dp"),
        P("dp"),
        P("dp", "mp"),
        P(("mp", "dp")),
        P("mp", "dp"),
        P("dp"),
        P("dp"),
    )
    return jax.shard_map(
        per_device, mesh=mesh, in_specs=in_specs, out_specs=out_specs, check_vma=False
    )
```

profile of v0, /device:TPU:0, one launch (start us, length us, event | category | flops | bytes accessed | tf_op | source)
XLA Modules:
  0.0 831.7 jit_solution(17333124179165116436)
XLA Ops:
  7.3 6.5 convolution_bitcast_fusion
  15.1 3.2 fusion.128
  18.7 4.0 convert_element_type.154
  22.7 5.6 squeeze.48
  28.3 5.6 squeeze.47
  34.0 6.5 fusion.30
  40.4 26.4 %while.14 = (s32[]{:T(128)}, bf16[4,2,256,6,64]{2,4,3,1,0:T(8,128)(2,1)}, f32[4,2,6]{2,1,0:T(2,128)S(1)}, bf16[4,2,256,6,64]{2,4,3,1,0:T(8,128)(2,1)}, pred[4,2,...) while((s32[]{:T(128)}, ...), condition=%wide.region_3.4_spmd, body=%wide.region_0.3_spmd.sunk | while | flops 210957312 | bytes 11900621 | solution.py:88
  41.7 1.8 fusion.156
  44.2 2.7 fusion.158
  48.3 1.8 fusion.156
  50.8 2.7 fusion.158
  54.9 1.8 fusion.156
  57.3 2.7 fusion.158
  61.5 1.8 fusion.156
  63.9 2.7 fusion.158
  66.8 4.2 copy.123
  71.0 3.8 reshape.346
  74.9 4.9 convolution_convert_fusion
  80.5 87.9 %all-reduce.13.cloned.1.call-done = bf16[2048,768]{1,0:T(8,128)(2,1)} async-done(((bf16[2048,768]{1,0:T(8,128)(2,1)}), bf16[2048,768]{1,0:T(8,128)(2,1)}) %all-reduce.13.cloned.1.call-update) | async-done | bytes 3145744 | tf_op jit(solution)/shard_map/psum | solution.py:100
  168.4 3.9 fusion.127
  173.2 1.7 copy-done.1
  176.1 32.5 %fusion.18 = (bf16[2048,1536]{1,0:T(8,128)(2,1)S(1)}, f32[2048,1536]{1,0:T(8,128)}) fusion(f32[1536]{0:T(1024)S(1)} %convert_element_type.161, bf16[2048,768]{1,0:T(8,128)(2,1)S(1)} %fusion.26, bf16[768,1536]{1,0:T(8,128)(2,1)S(1)} %copy-done), kind=kOutput, calls=%fused_computation.28 | convolution fusion | flops 5039456256 | bytes 24385536 | tf_op jit(solution)/shard_map/dot_general | solution.py:107
  208.6 2.6 copy-done.49
  211.3 6.4 convolution_convert_fusion.1
  218.2 3.3 copy.168
  222.8 2.3 copy.167
  225.3 1.7 slice.127
  227.0 3.1 copy.169
  230.1 3.1 copy.170
  233.5 1.9 fusion.41
  236.1 3.5 add_convert_fusion
  242.5 61.1 %all-reduce.15.cloned.1.call-done = bf16[2048,768]{1,0:T(8,128)(2,1)} async-done(((bf16[2048,768]{1,0:T(8,128)(2,1)}), bf16[2048,768]{1,0:T(8,128)(2,1)}) %all-reduce.15.cloned.1.call-update) | async-done | bytes 3145744 | tf_op jit(solution)/shard_map/psum | solution.py:111
  303.6 4.9 fusion.126
  309.4 1.8 copy-done.2
  312.1 1.7 copy-done.4
  313.8 21.9 %all-gather = bf16[128,1,768]{2,0,1:T(8,128)(2,1)S(1)} all-gather(bf16[8,1,768]{2,0,1:T(8,128)(2,1)S(1)} %copy.158), channel_id=2, replica_groups=mesh['dp'=16,'mp'=2] {'dp'}, dimensions={0}, use_global_device_ids=true | all-gather | bytes 208896 | tf_op jit(solution)/shard_map/all_gather | solution.py:121
  339.3 50.7 %reduce-scatter.9.cloned.1.call-done = f32[8,768]{1,0:T(8,128)} async-done(((f32[128,768]{1,0:T(8,128)}), f32[8,768]{1,0:T(8,128)}) %reduce-scatter.9.cloned.1.call-update) | async-done | bytes 24592 | tf_op jit(solution)/shard_map/reduce_scatter | solution.py:132
  392.4 2.4 fusion.131
  395.5 8.4 %psum.23 = f32[8,768]{1,0:T(8,128)S(1)} all-reduce(f32[8,768]{1,0:T(8,128)S(1)} %fusion.93), channel_id=1, replica_groups=mesh['dp'=16,'mp'=2] {'mp'}, use_global_device_ids=true, to_apply=%region_18.19 | all-reduce | flops 6144 | bytes 49152 | tf_op jit(solution)/shard_map/psum | solution.py:154
  406.8 1.9 fusion.37
  409.8 2.0 fusion.39
  412.0 2.4 bitcast_convert_fusion
  414.4 3.7 convert_element_type.183
  418.1 2.6 copy.133
  422.4 3.7 convert_element_type.180
  426.1 2.6 copy.132
  429.1 5.5 fusion.33
  434.6 2.0 pad_maximum_fusion
  436.6 6.3 copy.137
  443.0 4.9 fusion.32
  447.9 2.7 copy-done.5
  452.0 1.7 scatter-add.6
  453.7 4.8 convert_element_type.186
  458.5 4.7 copy.152
  467.2 3.0 fusion.85
  471.4 3.0 fusion.89
  478.6 2.7 dynamic-slice_convert_fusion
  482.6 58.6 %all-reduce.8 = (f32[2,384]{1,0:T(2,128)S(1)}, f32[768]{0:T(1024)S(1)}, f32[768]{0:T(1024)S(1)}, f32[768]{0:T(1024)S(1)}, f32[1536]{0:T(1024)S(1)}, /*index=5*/f32[768]{0:T(1024)S(1)}, f32[768]{0:T(1024)S(1)}) all-reduce(f32[2,384]{1,0:T(2,128)S(1)} %pad_maximum_fusion.6, ...), channel_id=6, replica_groups=mesh['dp'=16,'mp'=2] {'dp'}, use_global_device_ids=true, to_apply=%region_28.29.clone | all-reduce | flops 6144 | bytes 49152
  545.3 13.3 %all-reduce.17.cloned.1.call-done = f32[3,768,384]{2,0,1:T(4,128)} async-done(((f32[3,768,384]{2,0,1:T(4,128)}), f32[3,768,384]{2,0,1:T(4,128)}) %all-reduce.17.cloned.1.call-update) | async-done | bytes 3538960
  560.4 43.5 %reduce-scatter.17.cloned.1.call-done = bf16[384,2048]{1,0:T(8,128)(2,1)} async-done(((bf16[768,2048]{1,0:T(8,128)(2,1)}), bf16[384,2048]{1,0:T(8,128)(2,1)}) %reduce-scatter.17.cloned.1.call-update) | async-done | bytes 1572880
  603.9 2.6 copy.153
  611.4 54.7 %reduce-scatter.11.cloned.1.call-done = f32[384,48]{0,1:T(8,128)} async-done(((f32[384,768]{0,1:T(8,128)}), f32[384,48]{0,1:T(8,128)}) %reduce-scatter.11.cloned.1.call-update) | async-done | bytes 73744 | tf_op jit(solution)/shard_map/reduce_scatter | solution.py:216
  666.0 79.0 %reduce-scatter.15.cloned.1.call-done = f32[1536,48]{0,1:T(8,128)} async-done(((f32[1536,768]{0,1:T(8,128)}), f32[1536,48]{0,1:T(8,128)}) %reduce-scatter.15.cloned.1.call-update) | async-done | bytes 294928 | tf_op jit(solution)/shard_map/reduce_scatter | solution.py:222
  745.1 79.6 %reduce-scatter.13.cloned.1.call-done = f32[48,1536]{1,0:T(8,128)} async-done(((f32[768,1536]{1,0:T(8,128)}), f32[48,1536]{1,0:T(8,128)}) %reduce-scatter.13.cloned.1.call-update) | async-done | bytes 294928 | tf_op jit(solution)/shard_map/reduce_scatter | solution.py:220
  (231 shorter events, 53.9 us)
Async XLA Ops:
  7.2 168.9 %copy-start = (bf16[768,1536]{1,0:T(8,128)(2,1)S(1)}, bf16[768,1536]{1,0:T(8,128)(2,1)}, u32[]{:S(2)}) copy-start(bf16[768,1536]{1,0:T(8,128)(2,1)} %param.31) | copy-start | bytes 7077892
  7.2 161.2 %all-reduce.13.cloned.1.call-start = ((), (), s32[]{:S(2)}) async-start(), calls=%async_computation.5 | async-start | bytes 6291456 | tf_op jit(solution)/shard_map/psum | solution.py:100
  15.1 3.2 copy-start.45
  15.1 3.4 copy-start.47
  18.5 9.8 %copy-start.21 = (f32[384]{0:T(512)}, f32[384]{0:T(512)S(1)}, u32[]{:S(2)}) copy-start(f32[384]{0:T(512)S(1)} %get-tuple-element.196) | copy-start | bytes 4612
  18.6 15.3 %copy-start.19 = (f32[6,64]{1,0:T(8,128)}, f32[6,64]{1,0:T(8,128)S(1)}, u32[]{:S(2)}) copy-start(f32[6,64]{1,0:T(8,128)S(1)} %add.188) | copy-start | bytes 4612
  66.8 8.1 copy-start.9
  79.8 0.7 copy-start.40
  79.8 0.7 copy-start.41
  79.8 0.7 copy-start.42
  79.8 0.7 copy-start.38
  79.8 223.8 %all-reduce.15.cloned.1.call-start = ((), (), s32[]{:S(2)}) async-start(), calls=%async_computation.6 | async-start | bytes 6291456 | tf_op jit(solution)/shard_map/psum | solution.py:111
  172.4 2.6 copy-start.1
  176.1 32.5 %copy-start.6 = (bf16[2048,768]{1,0:T(8,128)(2,1)}, bf16[2048,768]{1,0:T(8,128)(2,1)S(1)}, u32[]{:S(2)}) copy-start(bf16[2048,768]{1,0:T(8,128)(2,1)S(1)} %fusion.26) | copy-start | bytes 9437188
  176.1 35.1 %copy-start.8 = (bf16[1536,768]{1,0:T(8,128)(2,1)S(1)}, bf16[1536,768]{1,0:T(8,128)(2,1)}, u32[]{:S(2)}) copy-start(bf16[1536,768]{1,0:T(8,128)(2,1)} %param.33) | copy-start | bytes 7077892
  208.6 2.6 copy-start.49
  217.7 172.3 %reduce-scatter.9.cloned.1.call-start = ((), (), s32[]{:S(2)}) async-start(), calls=%async_computation.7 | async-start | bytes 417792 | tf_op jit(solution)/shard_map/reduce_scatter | solution.py:132
  221.5 3.6 copy-start.22
  221.5 3.8 copy-start.43
  221.5 3.8 copy-start.44
  225.3 4.8 copy-start.3
  230.1 3.3 copy-start.50
  230.1 3.4 copy-start.46
  230.1 6.0 copy-start.20
  233.4 6.3 copy-start.24
  233.4 103.2 %copy-start.30 = (s32[12]{0:T(128)}, s32[12]{0:T(128)S(1)}, u32[]{:S(2)}) copy-start(s32[12]{0:T(128)S(1)} %dynamic_slice.24) | copy-start | bytes 148
  233.5 6.1 copy-start.29
  241.7 66.8 %copy-start.34 = (f32[8]{0:T(128)}, f32[8]{0:T(128)S(1)}, u32[]{:S(2)}) copy-start(f32[8]{0:T(128)S(1)} %broadcast_multiply_fusion.2) | copy-start | bytes 100
  241.9 66.6 %copy-start.48 = (f32[8]{0:T(128)}, f32[8]{0:T(128)S(1)}, u32[]{:S(2)}) copy-start(f32[8]{0:T(128)S(1)} %multiply_reduce_fusion.5) | copy-start | bytes 100
  308.5 2.7 copy-start.2
  311.2 24.5 %copy-start.17 = (bf16[12,768]{1,0:T(8,128)(2,1)S(1)}, bf16[12,768]{1,0:T(8,128)(2,1)}, u32[]{:S(2)}) copy-start(bf16[12,768]{1,0:T(8,128)(2,1)} %param.23) | copy-start | bytes 55300
  312.1 1.7 copy-start.4
  335.7 68.3 %copy-start.35 = (f32[8]{0:T(128)S(1)}, f32[8]{0:T(128)}, u32[]{:S(2)}) copy-start(f32[8]{0:T(128)} %copy-done.34) | copy-start | bytes 100
  335.7 68.3 %copy-start.39 = (f32[8]{0:T(128)S(1)}, f32[8]{0:T(128)}, u32[]{:S(2)}) copy-start(f32[8]{0:T(128)} %fusion.114) | copy-start | bytes 100
  336.7 69.9 %copy-start.32 = (f32[12]{0:T(128)}, f32[12]{0:T(128)S(1)}, u32[]{:S(2)}) copy-start(f32[12]{0:T(128)S(1)} %get-tuple-element.227) | copy-start | bytes 148
  337.9 220.7 %all-reduce.17.cloned.1.call-start = ((), (), s32[]{:S(2)}) async-start(), calls=%async_computation.12 | async-start | bytes 9437184
  392.3 16.3 %copy-start.11 = (f32[8,768]{1,0:T(8,128)}, f32[8,768]{1,0:T(8,128)S(1)}, u32[]{:S(2)}) copy-start(f32[8,768]{1,0:T(8,128)S(1)} %get-tuple-element.225) | copy-start | bytes 73732
  392.4 14.3 %copy-start.36 = (f32[8]{0:T(128)}, f32[8]{0:T(128)S(1)}, u32[]{:S(2)}) copy-start(f32[8]{0:T(128)S(1)} %negate_multiply_fusion.3) | copy-start | bytes 100
  394.8 17.0 %copy-start.15 = (bf16[8,1536]{1,0:T(8,128)(2,1)}, bf16[8,1536]{1,0:T(8,128)(2,1)S(1)}, u32[]{:S(2)}) copy-start(bf16[8,1536]{1,0:T(8,128)(2,1)S(1)} %get-tuple-element.250) | copy-start | bytes 73732
  406.3 5.5 copy-start.13
  422.4 6.3 copy-start.18
  443.0 160.9 %reduce-scatter.17.cloned.1.call-start = ((), (), s32[]{:S(2)}) async-start(), calls=%async_computation.11 | async-start | bytes 4718592
  447.9 2.7 copy-start.5
  463.3 1.5 copy-start.14
  463.3 3.9 copy-start.12
  463.3 3.9 copy-start.37
  463.3 202.7 %reduce-scatter.11.cloned.1.call-start = ((), (), s32[]{:S(2)}) async-start(), calls=%async_computation.8 | async-start | bytes 1253376 | tf_op jit(solution)/shard_map/reduce_scatter | solution.py:216
  466.2 278.9 %reduce-scatter.15.cloned.1.call-start = ((), (), s32[]{:S(2)}) async-start(), calls=%async_computation.10 | async-start | bytes 5013504 | tf_op jit(solution)/shard_map/reduce_scatter | solution.py:222
  470.2 1.2 copy-start.16
  470.3 354.4 %reduce-scatter.13.cloned.1.call-start = ((), (), s32[]{:S(2)}) async-start(), calls=%async_computation.9 | async-start | bytes 5013504 | tf_op jit(solution)/shard_map/reduce_scatter | solution.py:220
  474.5 0.7 copy-start.51
  474.5 3.2 copy-start.31
  474.5 3.2 copy-start.33
  474.5 6.9 copy-start.10
  474.5 8.0 copy-start.23
  474.5 8.0 copy-start.25
  474.5 8.0 copy-start.26
  474.5 8.0 copy-start.27
  474.5 8.0 copy-start.28
  608.1 1.7 copy-start.7
Sparse Core Ops, SparseCore 0:
  79.9 88.4 all-reduce.12
  217.8 85.7 all-reduce.14
  338.1 51.8 reduce-scatter.8
  443.1 115.5 all-reduce.16
  560.8 43.0 reduce-scatter.16
  607.9 58.0 reduce-scatter.10
  670.5 74.5 reduce-scatter.14
  750.0 74.5 reduce-scatter.12
where the time goes:
time: 838 us; the launch traced here: 832 us
  waiting for transfers between devices  470 us (56%)
  local copies, waits for them, and re-layouts  106 us (13%)
  matrix products  99.2 us (12%)
  blocking collectives  88.9 us (11%)
  other arithmetic  49.6 us (6%)
  between operations  17 us (2%)
    psum x1, waiting for transfers between devices, per_device(): lax.psum(partial_attn, 'mp').astype(jnp.float32) + b_out.astype(jnp.float32)  87.9 us
    reduce_scatter x1, waiting for transfers between devices, per_device(): lax.psum_scatter(grad_in, 'dp', scatter_dimension=0, tiled=True)  79.6 us
    reduce_scatter x1, waiting for transfers between devices, per_device(): lax.psum_scatter(grad_back, 'dp', scatter_dimension=1, tiled=True)  79 us
    psum x1, waiting for transfers between devices, per_device(): lax.psum(partial_ffn, 'mp').astype(jnp.float32)  61.1 us
    unnamed x1, blocking collectives  58.6 us
    unnamed x10, waiting for transfers between devices  57 us
    reduce_scatter x1, waiting for transfers between devices, per_device(): lax.psum_scatter(grad_out, 'dp', scatter_dimension=1, tiled=True)  54.7 us
    reduce_scatter x1, waiting for transfers between devices, per_device(): lax.psum_scatter(jnp.einsum('qp,qd->pd', slopes, queries_wide, precision=...  50.7 us
  transfers between devices with their start and end apart: 8, of which 8 were waited for; matrix products, arithmetic and copies ran while one was open for 9% of the time, Pallas kernels for 0%

commit v1 on v0

v1 whole, which is shorter than its diff:
```python
import functools
import math

import jax
import jax.numpy as jnp
from jax import lax
from jax.experimental import pallas as pl
from jax.experimental.pallas import tpu as pltpu
from jax.sharding import PartitionSpec as P

HEAD = 64
EPS = 1e-05
MASKED = -1e30
MESH = pl.DeviceIdType.MESH
BF = jnp.bfloat16
F32 = jnp.float32
MIB = 2**20


def nn(a, b):
    return jnp.dot(a, b, preferred_element_type=F32)


def nt(a, b):
    return lax.dot_general(a, b, (((1,), (1,)), ((), ())), preferred_element_type=F32)


def tn(a, b):
    return lax.dot_general(a, b, (((0,), (0,)), ((), ())), preferred_element_type=F32)


def gelu(h):
    return 0.5 * h * (1.0 + lax.erf(h * math.sqrt(0.5)))


def gelu_slope(h):
    bell = jnp.exp(-0.5 * h * h) * (1.0 / math.sqrt(2.0 * math.pi))
    return 0.5 * (1.0 + lax.erf(h * math.sqrt(0.5))) + h * bell


def standard(rows):
    center = jnp.mean(rows, axis=-1, keepdims=True)
    spread = rows - center
    second = jnp.mean(spread * spread, axis=-1, keepdims=True)
    inverse = lax.rsqrt(second + EPS)
    return spread * inverse, inverse


def norm_back(grad, scaled, inverse):
    first = jnp.mean(grad, axis=-1, keepdims=True)
    second = jnp.mean(grad * scaled, axis=-1, keepdims=True)
    return inverse * (grad - first - scaled * second)


def flip(index, bit):
    return index + bit * (1 - 2 * lax.rem(lax.div(index, bit), 2))


def mult(value, step):
    return pl.multiple_of(value, step)


def tower(
    nd,
    query_total,
    lengths,
    tokens,
    queries,
    positives,
    w_qkv,
    b_qv,
    w_out,
    b_out,
    gain_one,
    shift_one,
    w_in,
    b_in,
    w_back,
    b_back,
    gain_two,
    out_act,
    o_coef,
    o_rank,
    o_factor,
    o_dquery,
    o_active,
    o_inner,
    o_context,
    o_qcls,
    o_dctx,
    o_norm,
    o_ffn,
    o_attn,
    o_tok,
    o_sums,
    o_sums_in,
    o_loss,
    o_qgrad,
    tok,
    wq,
    wo,
    wi,
    wb,
    keyb,
    valb,
    ctx,
    ctx_send,
    norm_low,
    acc,
    act_far,
    obuf,
    chance,
    factor,
    stage,
    tcls,
    pack,
    gath,
    ctx_all,
    tok_all,
    q_all,
    xh1_all,
    norm_all,
    inner_all,
    act_all,
    low_all,
    dc_all,
    qc_all,
    d1_all,
    dq_rows,
    rank_f,
    coef_own,
    coef_far,
    rank_own,
    rank_send,
    rank_far,
    fac_send,
    fac_all,
    dq_send,
    dq_all,
    loc_sem,
    ysend,
    yrecv,
    w_send,
    w_recv,
    c_send,
    c_recv,
    o_send,
    o_recv,
    o_loc,
    g_send,
    g_recv,
    gs_send,
    gs_recv,
    f_send,
    f_recv,
    q_send,
    q_recv,
    m_send,
    m_recv,
    b_send,
    b_recv,
    bin_own,
    bin_far,
):
    dp = lax.axis_index("dp")
    mp = lax.axis_index("mp")
    far = 1 - mp
    chips = nd // 2
    core = lax.rem(dp, 2)
    chip = lax.div(dp, 2)
    bit_a = lax.rem(lax.div(dp, 2), 2)
    bit_b = lax.rem(lax.div(dp, 4), 2)
    quarter = bit_a + 2 * bit_b
    quarter_x = flip(quarter, 1)
    quarter_z = flip(quarter, 2)
    quarter_d = 3 - quarter
    pair = (dp, far)
    sibling = (flip(dp, 1), mp)
    near_x = (flip(dp, 2), mp)
    near_z = (flip(dp, 4), mp)

    rows, width = tok.shape
    count = lengths.shape[0]
    slot = rows // count
    own = count // 2
    half = width // 2
    own_rows = own * slot
    passages = nd * count
    blocks, unit = wi.shape[1], wi.shape[3]
    m_col = mult(mp * half, 128)
    f_col = mult(far * half, 128)

    barrier = pltpu.get_barrier_semaphore()

    def greet(i, carry):
        other = lax.rem(dp * 2 + mp + i, 2 * nd)
        pl.semaphore_signal(
            barrier,
            inc=1,
            device_id=(lax.div(other, 2), lax.rem(other, 2)),
            device_id_type=MESH,
        )
        return carry

    lax.fori_loop(1, 2 * nd, greet, 0)

    def local(src, dst, k):
        return pltpu.make_async_copy(src, dst, loc_sem.at[k])

    loads = [local(tokens, tok, 0)]
    loads += [local(w_qkv.at[j], wq.at[:, pl.ds(j * half, half)], 1 + j) for j in range(3)]
    loads.append(local(w_out, wo.at[pl.ds(mult(mp * half, 128), half), :], 4))
    loads += [
        local(w_in.at[:, pl.ds(u * unit, unit)], wi.at[mp, u], 5 + u) for u in range(blocks)
    ]
    loads += [
        local(w_back.at[pl.ds(u * unit, unit), :], wb.at[mp, u], 5 + blocks + u)
        for u in range(blocks)
    ]
    for copy in loads:
        copy.start()

    chunks = 1 + 2 * blocks

    def piece(k, q, c, which, side=None):
        if k == 0:
            size = half // 8
            at = mult(which * half + (c * 4 + q) * size, 16)
            cols = pl.ds(0, width) if side is None else pl.ds(side * half, half)
            return wo.at[pl.ds(at, size), cols]
        if k <= blocks:
            size = width // 8
            at = (c * 4 + q) * size
            if side is not None:
                size = size // 2
                at = at + side * size
            return wi.at[which, k - 1, pl.ds(mult(at, 16), size), :]
        size = unit // 8
        cols = pl.ds(0, width) if side is None else pl.ds(side * half, half)
        return wb.at[which, k - 1 - blocks, pl.ds(mult((c * 4 + q) * size, 16), size), cols]

    def source(k):
        if k == 0:
            size = half // 8
            return w_out.at[pl.ds(mult((core * 4 + quarter) * size, 16), size), :]
        if k <= blocks:
            size = width // 8
            at = mult((core * 4 + quarter) * size, 16)
            return w_in.at[pl.ds(at, size), pl.ds((k - 1) * unit, unit)]
        size = unit // 8
        at = mult((k - 1 - blocks) * unit + (core * 4 + quarter) * size, 16)
        return w_back.at[pl.ds(at, size), :]

    def remote(src, dst, ss, rs, device):
        return pltpu.make_async_remote_copy(
            src_ref=src,
            dst_ref=dst,
            send_sem=ss,
            recv_sem=rs,
            device_id=device,
            device_id_type=MESH,
        )

    def cross(k):
        return remote(
            source(k), piece(k, quarter, core, mp), ysend.at[k], yrecv.at[k], pair
        )

    def send(k, lane, q, c, side, device):
        ref = piece(k, q, c, far, side)
        return remote(ref, ref, w_send.at[k, lane], w_recv.at[k, lane], device)

    def lane(k, n):
        q = (quarter, quarter, quarter_z, quarter_x, quarter, quarter_x, quarter_z, quarter_d)[n]
        side = (None, None, 0, 1, None, None, None, None)[n]
        return send(k, n, q, core, side, (near_x, near_z, near_x, near_z)[n] if n < 4 else sibling)

    def arrival(k, n):
        q = (quarter_x, quarter_z, quarter_d, quarter_d, quarter, quarter_x, quarter_z, quarter_d)[n]
        side = (None, None, 0, 1, None, None, None, None)[n]
        c = core if n < 4 else 1 - core
        return send(k, n, q, c, side, (near_x, near_z, near_x, near_z)[n] if n < 4 else sibling)

    def step_one(k):
        remote(
            source(k), piece(k, quarter, core, far), ysend.at[k], yrecv.at[k], pair
        ).wait_recv()
        for n in (0, 1, 4):
            lane(k, n).start()

    def step_two(k):
        arrival(k, 1).wait_recv()
        lane(k, 2).start()
        arrival(k, 0).wait_recv()
        for n in (3, 5, 6):
            lane(k, n).start()

    def step_three(k):
        arrival(k, 2).wait_recv()
        arrival(k, 3).wait_recv()
        lane(k, 7).start()

    def complete(k):
        for n in range(4, 8):
            arrival(k, n).wait_recv()

    def tick(i):
        if i < chunks:
            step_one(i)
        if 0 <= i - 1 < chunks:
            step_two(i - 1)
        if 0 <= i - 2 < chunks:
            step_three(i - 2)

    for copy in loads[:4]:
        copy.wait()
    pl.semaphore_wait(barrier, 2 * nd - 1)
    bin_own[...] = jnp.zeros_like(bin_own)
    bin_own[0:blocks, :] = b_in[...].astype(F32)
    bias_copy = remote(bin_own, bin_far, b_send, b_recv, pair)
    bias_copy.start()
    for k in range(chunks):
        cross(k).start()

    lane_pair = lax.broadcasted_iota(jnp.int32, (slot, 128), 1)
    key_place = lax.broadcasted_iota(jnp.int32, (1, slot), 1)
    head_rows = lax.broadcasted_iota(jnp.int32, (8, half), 0)
    head_mask = head_rows == lax.div(lax.broadcasted_iota(jnp.int32, (8, half), 1), HEAD)
    heads = half // HEAD
    live = lax.broadcasted_iota(jnp.int32, (8, 1), 0) < heads
    bias_q = b_qv[0:1, :].astype(F32)
    bias_v = b_qv[1:2, :].astype(F32)
    ones = jnp.ones((slot, 128), BF)
    row_place = lax.broadcasted_iota(jnp.int32, (8, slot), 0)
    first_key = (lax.broadcasted_iota(jnp.int32, (8, slot), 1) == 0).astype(F32)

    def ctx_copy(i):
        there = ctx.at[pl.ds(mult(i * slot, 16), slot), pl.ds(m_col, half)]
        return remote(
            ctx_send.at[pl.ds(mult(i * slot, 16), slot), :], there, c_send.at[i], c_recv.at[i], pair
        )

    def ctx_came(i):
        here = ctx.at[pl.ds(mult(i * slot, 16), slot), pl.ds(f_col, half)]
        return remote(
            ctx_send.at[pl.ds(mult(i * slot, 16), slot), :], here, c_send.at[i], c_recv.at[i], pair
        )

    def attend(i, carry):
        theirs = i < own
        side = jnp.where(theirs, far, mp)
        place = lax.rem(i, own)
        p = side * own + place
        at = mult(p * slot, slot)
        x = tok[pl.ds(at, slot), :]
        made = nn(x, wq[...])
        query = ((made[:, :half] + bias_q).astype(BF).astype(F32) * 0.125).astype(BF)
        keyed = made[:, half : 2 * half].astype(BF)
        value = (made[:, 2 * half :] + bias_v).astype(BF)
        keyb[pl.ds(at, slot), :] = keyed
        valb[pl.ds(at, slot), :] = value
        length = lengths[p]
        bias = jnp.where(key_place < length, 0.0, MASKED)
        done = []
        for t in range(half // 128):
            q2 = query[:, 128 * t : 128 * t + 128]
            k2 = keyed[:, 128 * t : 128 * t + 128]
            v2 = jnp.concatenate([value[:, 128 * t : 128 * t + 128], ones], axis=1)
            parts = []
            for hx in range(2):
                mask = (lane_pair < HEAD) if hx == 0 else (lane_pair >= HEAD)
                s = nt(jnp.where(mask, q2, jnp.zeros_like(q2)), k2) + bias
                e = jnp.exp(s - jnp.max(s, axis=1, keepdims=True)).astype(BF)
                o = nn(e, v2)
                parts.append(o[:, :128] / o[:, 128:])
            done.append(jnp.where(lane_pair < HEAD, parts[0], parts[1]))
        mixed = jnp.concatenate(done, axis=1)
        low = mixed.astype(BF)
        stage[pl.ds(p, 1), :] = mixed[0:1, :]
        tcls[pl.ds(p, 1), :] = x[0:16, :].astype(F32)[0:1, :]
        q_row = query[0:16, :].astype(F32)[0:1, :]
        q_heads = jnp.where(head_mask, q_row, 0.0).astype(BF)
        s = nt(q_heads, keyed) + bias
        e = jnp.exp(s - jnp.max(s, axis=1, keepdims=True))
        c = jnp.where(live, e / jnp.sum(e, axis=1, keepdims=True), 0.0)
        chance[p] = c
        c_low = c.astype(BF)
        coef_own[pl.ds(mult(p * 16, 16), 8), :] = jnp.where(row_place == heads, first_key, c)
        factor[pl.ds(mult(p * 8, 8), 8), :] = nn(c_low, x)

        @pl.when(theirs)
        def _():
            ctx_send[pl.ds(mult(place * slot, 16), slot), :] = low
            ctx_copy(place).start()

        @pl.when(i >= own)
        def _():
            ctx[pl.ds(mult(place * slot, 16), slot), pl.ds(m_col, half)] = low

        @pl.when(i == own)
        def _():
            tick(0)

        @pl.when(i == own + 2)
        def _():
            tick(1)

        return carry

    lax.fori_loop(0, count, attend, 0)

    pack[0:8, :] = stage[...]
    pack[8:16, :] = tcls[:, pl.ds(m_col, half)]
    pack[16:32, :] = jnp.zeros((16, half), F32)
    q_rows = queries.shape[0]
    pack[16 : 16 + q_rows, :] = queries[:, pl.ds(m_col, half)].astype(F32)
    gath[chip, core, mp] = pack[...].astype(BF)

    def gather_copy(i, mine):
        me = chip * 2 + mp
        there = lax.rem(me + i, 2 * chips)
        t_chip, t_mp = lax.div(there, 2), lax.rem(there, 2)
        holder = gath.at[chip, core, mp] if mine else gath.at[t_chip, core, t_mp]
        return remote(
            gath.at[chip, core, mp],
            holder,
            g_send.at[i],
            g_recv.at[me if mine else there],
            (t_chip * 2 + core, t_mp),
        )

    def gather_start(i, carry):
        gather_copy(i, True).start()
        return carry

    def gather_wait(i, carry):
        gather_copy(i, False).wait_recv()
        return carry

    def gather_sent(i, carry):
        gather_copy(i, True).wait_send()
        return carry

    lax.fori_loop(1, 2 * chips, gather_start, 0)

    for copy in loads[4:]:
        copy.wait()
    tick(2)
    tick(3)
    complete(0)
    bo = b_out[0:1, :].astype(F32)
    g1 = gain_one[0:1, :].astype(F32)
    s1 = shift_one[0:1, :].astype(F32)
    g2 = gain_two[0:1, :].astype(F32)
    bb = b_back[0:1, :].astype(F32)

    def feed_own(i, carry):
        ctx_came(i).wait_recv()
        at = mult(i * slot, slot)
        here = pl.ds(at, slot)
        x = tok[pl.ds(mult(mp * own_rows + i * slot, slot), slot), :].astype(F32)
        resid = x + nn(ctx[here, :], wo[...]) + bo
        scaled, _ = standard(resid)
        norm = scaled * g1 + s1
        low = norm.astype(BF)
        norm_low[here, :] = low
        total = norm + bb
        for u in range(blocks):
            inner = nn(low, wi[mp, u]) + bin_own[u : u + 1, :]
            total = total + nn(gelu(inner).astype(BF), wb[mp, u])
        acc[here, :] = total

        for j in range(own):

            @pl.when(i == j)
            def _():
                if j + 4 < chunks + 2:
                    tick(j + 4)

        return carry

    lax.fori_loop(0, own, feed_own, 0)
    for i in range(own + 4, chunks + 2):
        tick(i)

    lax.fori_loop(1, 2 * chips, gather_wait, 0)
    to_sibling = remote(gath.at[:, core], gath.at[:, core], gs_send, gs_recv, sibling)
    to_sibling.start()

    bias_copy.wait_recv()
    for u in range(blocks):
        complete(1 + u)

        def feed_far_in(i, carry, u=u):
            here = pl.ds(mult(i * slot, slot), slot)
            inner = nn(norm_low[here, :], wi[far, u]) + bin_far[u : u + 1, :]
            act_far[u, here, :] = gelu(inner).astype(BF)
            return carry

        lax.fori_loop(0, own, feed_far_in, 0)

    for u in range(blocks - 1):
        complete(1 + blocks + u)

        def feed_far_back(i, carry, u=u):
            here = pl.ds(mult(i * slot, slot), slot)
            acc[here, :] += nn(act_far[u, here, :], wb[far, u])
            return carry

        lax.fori_loop(0, own, feed_far_back, 0)

    complete(chunks - 1)

    def out_copy(i, mine):
        side = mp if mine else far
        there = out_act.at[pl.ds(mult(side * own_rows + i * slot, 16), slot), :]
        return remote(
            obuf.at[1, pl.ds(mult(i * slot, 16), slot), :], there, o_send.at[i], o_recv.at[i], pair
        )

    def out_local(i):
        there = out_act.at[pl.ds(mult(mp * own_rows + i * slot, 16), slot), :]
        return pltpu.make_async_copy(
            obuf.at[0, pl.ds(mult(i * slot, 16), slot), :], there, o_loc.at[i]
        )

    def finish(i, carry):
        here = pl.ds(mult(i * slot, slot), slot)
        total = acc[here, :] + nn(act_far[blocks - 1, here, :], wb[far, blocks - 1])
        scaled, _ = standard(total)
        acc[here, :] = scaled * g2
        obuf[0, here, :] = acc[here, pl.ds(m_col, half)].astype(BF)
        obuf[1, here, :] = acc[here, pl.ds(f_col, half)].astype(BF)
        out_copy(i, True).start()
        out_local(i).start()
        return carry

    lax.fori_loop(0, own, finish, 0)

    remote(
        gath.at[:, 1 - core], gath.at[:, 1 - core], gs_send, gs_recv, sibling
    ).wait_recv()
    q_pad = nd * 16
    for h in range(2):
        cols = slice(h * half, (h + 1) * half)
        block = gath[:, :, h].astype(F32)
        ctx_all[:, cols] = block[:, :, 0:8].reshape(passages, half).astype(BF)
        tok_all[:, cols] = block[:, :, 8:16].reshape(passages, half).astype(BF)
        q_all[:, cols] = block[:, :, 16:32].reshape(q_pad, half).astype(BF)

    resid = tok_all[...].astype(F32) + nn(ctx_all[...], wo[...]) + bo
    scaled, inverse1 = standard(resid)
    xh1_all[...] = scaled
    norm = scaled * g1 + s1
    low = norm.astype(BF)
    norm_all[...] = low
    total = norm + bb
    for h in range(2):
        for u in range(blocks):
            bias = jnp.where(mp == h, bin_own[u : u + 1, :], bin_far[u : u + 1, :])
            inner = nn(low, wi[h, u]) + bias
            inner_all[h, u] = inner
            active = gelu(inner).astype(BF)
            act_all[h, u] = active
            total = total + nn(active, wb[h, u])
    xh2, inverse2 = standard(total)
    cls = (xh2 * g2).astype(BF)
    similar = nt(cls, q_all[...])
    top = jnp.max(similar, axis=0, keepdims=True)
    log_sum = top + jnp.log(jnp.sum(jnp.exp(similar - top), axis=0, keepdims=True))
    target = lax.broadcasted_iota(jnp.int32, similar.shape, 0) == positives[0:1, :]
    picked = jnp.sum(jnp.where(target, similar, 0.0), axis=0, keepdims=True)
    o_loss[...] = jnp.broadcast_to(log_sum - picked, o_loss.shape)
    slopes = (jnp.exp(similar - log_sum) - target.astype(F32)) * (1.0 / query_total)
    slope_high = slopes.astype(BF)
    slope_low = (slopes - slope_high.astype(F32)).astype(BF)
    cls_grad = nn(slope_high, q_all[...]) + nn(slope_low, q_all[...])
    pick = (
        lax.broadcasted_iota(jnp.int32, (16, q_pad), 1)
        == lax.broadcasted_iota(jnp.int32, (16, q_pad), 0) + dp * 16
    ).astype(BF)
    o_qgrad[...] = nn(nt(pick, slope_high).astype(BF), cls) + nn(
        nt(pick, slope_low).astype(BF), cls
    )
    d_two = norm_back(g2 * cls_grad, xh2, inverse2)
    o_sums[0:1, :] = jnp.sum(cls_grad * xh2, axis=0, keepdims=True)
    o_sums[1:2, :] = jnp.sum(d_two, axis=0, keepdims=True)
    ffn_low = d_two.astype(BF)
    o_ffn[...] = ffn_low
    back = d_two
    for h in range(2):
        for u in range(blocks):
            d_active = nt(ffn_low, wb[h, u])
            d_inner = d_active * gelu_slope(inner_all[h, u])
            inner_all[h, u, 0:8, :] = jnp.broadcast_to(
                jnp.sum(d_inner, axis=0, keepdims=True), (8, unit)
            )
            inner_low = d_inner.astype(BF)
            low_all[h, u] = inner_low
            back = back + nt(inner_low, wi[h, u])
    for u in range(blocks):
        o_active[u] = act_all[mp, u]
        o_inner[u] = low_all[mp, u]
        o_sums_in[u : u + 1, :] = inner_all[mp, u, 0:1, :]
    xh1 = xh1_all[...]
    d_one = norm_back(g1 * back, xh1, inverse1)
    d1_all[...] = d_one
    o_sums[2:3, :] = jnp.sum(back * xh1, axis=0, keepdims=True)
    o_sums[3:4, :] = jnp.sum(back, axis=0, keepdims=True)
    o_sums[4:5, :] = jnp.sum(d_one, axis=0, keepdims=True)
    attn_low = d_one.astype(BF)
    o_attn[...] = attn_low
    o_norm[...] = norm_all[...]
    o_tok[...] = tok_all[...]
    d_ctx = nt(attn_low, wo[pl.ds(mult(mp * half, 128), half), :]).astype(BF)
    o_dctx[...] = d_ctx
    dc_all[...] = d_ctx.astype(F32)
    q_cls = (nn(tok_all[...], wq[:, 0:half]) + bias_q).astype(BF)
    o_qcls[...] = q_cls
    qc_all[...] = q_cls.astype(F32) * 0.125
    o_context[...] = ctx_all[:, pl.ds(m_col, half)]
    o_sums[5:6, 0:half] = jnp.sum(dc_all[...], axis=0, keepdims=True)

    base = mult(dp * count, 8)
    fkind = count * 8

    def attend_back(p, carry):
        at = mult(p * slot, slot)
        d_row = dc_all[pl.ds(base + p, 1), :]
        q_row = qc_all[pl.ds(base + p, 1), :]
        d_heads = jnp.where(head_mask, d_row, 0.0)
        q_heads = jnp.where(head_mask, q_row, 0.0)
        c = chance[p]
        d_chance = nt(d_heads.astype(BF), valb[pl.ds(at, slot), :])
        d_scores = c * (d_chance - jnp.sum(c * d_chance, axis=1, keepdims=True))
        s_low = d_scores.astype(BF)
        mark = jnp.logical_or(row_place == heads, row_place == heads + 1)
        coef_own[pl.ds(mult(p * 16 + 8, 8), 8), :] = jnp.where(mark, first_key, d_scores)
        factor[pl.ds(mult(fkind + p * 8, 8), 8), :] = nn(s_low, tok[pl.ds(at, slot), :])
        spread = nn(s_low, keyb[pl.ds(at, slot), :])
        dq_rows[pl.ds(p, 1), :] = 0.125 * jnp.sum(
            jnp.where(head_mask, spread, 0.0), axis=0, keepdims=True
        )
        rank_f[pl.ds(mult(p * 16, 8), 8), 0:half] = d_heads
        rank_f[pl.ds(mult(p * 16 + 8, 8), 8), 0:half] = q_heads
        return carry

    lax.fori_loop(0, count, attend_back, 0)

    turned = jnp.transpose(factor[...]).astype(BF)
    fac_send[...] = turned
    dq = dq_rows[...]
    for b in range(half // 128):
        pack[b * 8 : b * 8 + 8, 0:128] = dq[:, b * 128 : b * 128 + 128]
    pack[half // 16 : 32, 0:128] = jnp.zeros((32 - half // 16, 128), F32)
    dq_send[...] = pack[:, 0:128].astype(BF)
    share = width // nd
    fac_all[dp] = fac_send[pl.ds(mult(dp * share, 16), share), :]
    dq_all[dp] = dq_send[...]

    def factor_copy(i, mine):
        there = lax.rem(dp + i, nd)
        holder = fac_all.at[dp] if mine else fac_all.at[there]
        rows_out = fac_send.at[pl.ds(mult(there * share, 16), share), :]
        return remote(
            rows_out, holder, f_send.at[i], f_recv.at[dp if mine else there], (there, mp)
        )

    def dq_copy(i, mine):
        there = lax.rem(dp + i, nd)
        holder = dq_all.at[dp] if mine else dq_all.at[there]
        return remote(
            dq_send, holder, q_send.at[i], q_recv.at[dp if mine else there], (there, mp)
        )

    def factor_start(i, carry):
        factor_copy(i, True).start()
        dq_copy(i, True).start()
        return carry

    lax.fori_loop(1, nd, factor_start, 0)

    kept = rank_f[:, 0:half].astype(BF)
    even = lax.rem(lax.div(lax.broadcasted_iota(jnp.int32, (count * 16, 1), 0), 8), 2) == 0
    rank_v = nt(kept, wq[:, 2 * half :])
    rank_k = nt(kept, wq[:, half : 2 * half])
    rank_f[...] = jnp.where(even, rank_v, rank_k)
    back_q = nt(dq.astype(BF), wq[:, 0:half])
    for p in range(count):
        rank_f[p * 16 + heads : p * 16 + heads + 1, :] = back_q[p : p + 1, :]
        rank_f[p * 16 + heads + 1 : p * 16 + 8, :] = jnp.zeros((7 - heads, width), F32)
        rank_f[p * 16 + 8 + heads : p * 16 + 16, :] = jnp.zeros((8 - heads, width), F32)
    rank_send[...] = rank_f[:, pl.ds(f_col, half)].astype(BF)
    coef_low = coef_own[...].astype(BF)
    o_coef[0] = coef_low
    coef_far_copy = remote(o_coef.at[0], coef_far, m_send.at[0], m_recv.at[0], pair)
    coef_far_copy.start()
    rank_copy = remote(rank_send, rank_far, m_send.at[1], m_recv.at[1], pair)
    rank_copy.start()
    d1_rows = d1_all[pl.ds(base, count), pl.ds(m_col, half)]
    d1_high = d1_rows.astype(BF).astype(F32)
    d1_low = d1_rows - d1_high
    for p in range(count):
        rank_f[p * 16 + 8 + heads : p * 16 + 9 + heads, pl.ds(m_col, half)] = d1_high[p : p + 1]
        rank_f[p * 16 + 9 + heads : p * 16 + 10 + heads, pl.ds(m_col, half)] = d1_low[p : p + 1]
    o_rank[0] = rank_f[:, pl.ds(m_col, half)].astype(BF)

    coef_far_copy.wait_recv()
    rank_copy.wait_recv()
    o_coef[1] = coef_far[...]
    o_rank[1] = rank_far[...]

    def factor_wait(i, carry):
        factor_copy(i, False).wait_recv()
        dq_copy(i, False).wait_recv()
        return carry

    lax.fori_loop(1, nd, factor_wait, 0)
    o_factor[...] = fac_all[...]
    o_dquery[...] = dq_all[...]

    def factor_sent(i, carry):
        factor_copy(i, True).wait_send()
        dq_copy(i, True).wait_send()
        return carry

    lax.fori_loop(1, nd, factor_sent, 0)
    coef_far_copy.wait_send()
    rank_copy.wait_send()
    bias_copy.wait_send()
    lax.fori_loop(1, 2 * chips, gather_sent, 0)
    to_sibling.wait_send()
    for k in range(chunks):
        cross(k).wait_send()
        for n in range(8):
            lane(k, n).wait_send()

    def drain(i, carry):
        ctx_copy(i).wait_send()
        out_copy(i, True).wait_send()
        out_copy(i, False).wait_recv()
        out_local(i).wait()
        return carry

    lax.fori_loop(0, own, drain, 0)


def gradients(
    nd,
    act_in,
    coef,
    rank,
    factor,
    dquery,
    active,
    inner,
    context,
    qcls,
    dctx,
    norm,
    ffn,
    attn,
    tok,
    sums,
    sums_in,
    loss,
    act_out,
    input_grad,
    grad_qkv,
    grad_out,
    grad_in,
    grad_back,
    small,
    act_sem,
    wide,
    rhs,
):
    dp = lax.axis_index("dp")
    mp = lax.axis_index("mp")
    copy = pltpu.make_async_copy(act_in, act_out, act_sem)
    copy.start()
    passages, width = ffn.shape
    half = width // 2
    heads = half // HEAD
    share = width // nd
    count = passages // nd
    slot = coef.shape[2]

    def input_rows(p, carry):
        rows16 = pl.ds(mult(p * 16, 16), 16)
        at = pl.ds(mult(p * slot, slot), slot)
        both = jnp.concatenate([coef[0, rows16, :], coef[1, rows16, :]], axis=0)
        right = jnp.concatenate([rank[0, rows16, :], rank[1, rows16, :]], axis=0)
        input_grad[at, :] = tn(both, right)
        return carry

    lax.fori_loop(0, count, input_rows, 0)

    own = lax.broadcasted_iota(jnp.int32, (width, share), 0)
    pick = (own == lax.broadcasted_iota(jnp.int32, (width, share), 1) + dp * share).astype(BF)
    own_t = lax.broadcasted_iota(jnp.int32, (share, width), 1)
    pick_t = (own_t == lax.broadcasted_iota(jnp.int32, (share, width), 0) + dp * share).astype(BF)
    ffn_own = nn(ffn[...], pick).astype(BF)
    attn_own = nn(attn[...], pick).astype(BF)
    norm_own = nt(pick_t, norm[...]).astype(BF)
    tok_own = nt(pick_t, tok[...]).astype(BF)
    grad_out[...] = tn(context[...], attn_own)
    unit = active.shape[2]
    for u in range(active.shape[0]):
        grad_back[u * unit : (u + 1) * unit, :] = tn(active[u], ffn_own)
        grad_in[:, u * unit : (u + 1) * unit] = nn(norm_own, inner[u])

    spread = lax.broadcasted_iota(jnp.int32, (8, half), 0) == lax.div(
        lax.broadcasted_iota(jnp.int32, (8, half), 1), HEAD
    )
    fkind = count * 8

    def build(s, carry):
        wide[...] = qcls[pl.ds(mult(s * count, 8), count), :].astype(F32) * 0.125
        d_rows = dctx[pl.ds(mult(s * count, 8), count), :].astype(F32)
        q_rows = wide[...]
        k_blocks = [
            jnp.where(spread, q_rows[p : p + 1, :], 0.0) for p in range(count)
        ]
        v_blocks = [
            jnp.where(spread, d_rows[p : p + 1, :], 0.0) for p in range(count)
        ]
        rhs[pl.ds(mult(s * fkind, 16), fkind), 0:half] = jnp.concatenate(k_blocks, 0).astype(BF)
        rhs[pl.ds(mult(s * fkind, 16), fkind), half:] = jnp.concatenate(v_blocks, 0).astype(BF)
        return carry

    lax.fori_loop(0, nd, build, 0)
    grad_k = jnp.zeros((share, half), F32)
    grad_v = jnp.zeros((share, half), F32)
    for s in range(0, nd, 4):
        left_v = jnp.concatenate([factor[s + t][:, 0:fkind] for t in range(4)], axis=1)
        left_k = jnp.concatenate([factor[s + t][:, fkind:] for t in range(4)], axis=1)
        grad_k = grad_k + nn(left_k, rhs[s * fkind : (s + 4) * fkind, 0:half])
        grad_v = grad_v + nn(left_v, rhs[s * fkind : (s + 4) * fkind, half:])
    grad_qkv[1] = grad_k
    grad_qkv[2] = grad_v
    dq_sum = []
    grad_q = []
    for b in range(half // 128):
        cols = dquery[:, pl.ds(0, 32), :].astype(F32)[:, b * 8 : b * 8 + 8, :]
        cols = cols.reshape(passages, 128)
        dq_sum.append(jnp.sum(cols, axis=0, keepdims=True))
        grad_qkv[0, :, b * 128 : b * 128 + 128] = nn(tok_own, cols.astype(BF))
    small[0:8, :] = sums[...]
    small[8:9, 0:half] = jnp.concatenate(dq_sum, axis=1)
    small[9:16, :] = jnp.zeros((7, width), F32)
    copy.wait()


def per_device(nd, *arrays):
    (
        tokens,
        lengths,
        queries,
        positives,
        w_qkv,
        b_qv,
        w_out,
        b_out,
        gain_one,
        shift_one,
        w_in,
        b_in,
        w_back,
        b_back,
        gain_two,
    ) = arrays
    rows, width = tokens.shape
    count = lengths.shape[0]
    slot = rows // count
    half = w_qkv.shape[2]
    units = w_in.shape[1]
    unit = 512
    blocks = units // unit
    chunks = 1 + 2 * blocks
    own_rows = rows // 2
    passages = nd * count
    chips = nd // 2
    q_rows = queries.shape[0]
    q_pad = nd * 16
    share = width // nd
    dp = lax.axis_index("dp")
    mp = lax.axis_index("mp")

    places = jnp.pad(positives.reshape(nd, q_rows), ((0, 0), (0, 16 - q_rows)), constant_values=-1)
    vmem = pl.BlockSpec(memory_space=pltpu.VMEM)
    hbm = pl.BlockSpec(memory_space=pl.ANY)
    smem = pl.BlockSpec(memory_space=pltpu.SMEM)
    in_specs = [smem, hbm, vmem, vmem, hbm, vmem, hbm, vmem, vmem, vmem, hbm, vmem, hbm, vmem, vmem]
    shape = jax.ShapeDtypeStruct
    outs = [
        (shape((rows, half), BF), hbm),
        (shape((2, count * 16, slot), BF), vmem),
        (shape((2, count * 16, half), BF), vmem),
        (shape((nd, share, 128), BF), vmem),
        (shape((nd, 32, 128), BF), vmem),
        (shape((blocks, passages, unit), BF), vmem),
        (shape((blocks, passages, unit), BF), vmem),
        (shape((passages, half), BF), vmem),
        (shape((passages, half), BF), vmem),
        (shape((passages, half), BF), vmem),
        (shape((passages, width), BF), vmem),
        (shape((passages, width), BF), vmem),
        (shape((passages, width), BF), vmem),
        (shape((passages, width), BF), vmem),
        (shape((8, width), F32), vmem),
        (shape((8, unit), F32), vmem),
        (shape((8, q_pad), F32), vmem),
        (shape((16, width), F32), vmem),
    ]
    dma = pltpu.SemaphoreType.DMA
    scratch = [
        pltpu.VMEM((rows, width), BF),
        pltpu.VMEM((width, 3 * half), BF),
        pltpu.VMEM((width, width), BF),
        pltpu.VMEM((2, blocks, width, unit), BF),
        pltpu.VMEM((2, blocks, unit, width), BF),
        pltpu.VMEM((rows, half), BF),
        pltpu.VMEM((rows, half), BF),
        pltpu.VMEM((own_rows, width), BF),
        pltpu.VMEM((own_rows, half), BF),
        pltpu.VMEM((own_rows, width), BF),
        pltpu.VMEM((own_rows, width), F32),
        pltpu.VMEM((blocks, own_rows, unit), BF),
        pltpu.VMEM((2, own_rows, half), BF),
        pltpu.VMEM((count, 8, slot), F32),
        pltpu.VMEM((2 * count * 8, width), F32),
        pltpu.VMEM((8, half), F32),
        pltpu.VMEM((8, width), F32),
        pltpu.VMEM((32, half), F32),
        pltpu.VMEM((chips, 2, 2, 32, half), BF),
        pltpu.VMEM((passages, width), BF),
        pltpu.VMEM((passages, width), BF),
        pltpu.VMEM((q_pad, width), BF),
        pltpu.VMEM((passages, width), F32),
        pltpu.VMEM((passages, width), BF),
        pltpu.VMEM((2, blocks, passages, unit), F32),
        pltpu.VMEM((2, blocks, passages, unit), BF),
        pltpu.VMEM((2, blocks, passages, unit), BF),
        pltpu.VMEM((passages, half), F32),
        pltpu.VMEM((passages, half), F32),
        pltpu.VMEM((passages, width), F32),
        pltpu.VMEM((8, half), F32),
        pltpu.VMEM((count * 16, width), F32),
        pltpu.VMEM((count * 16, slot), F32),
        pltpu.VMEM((count * 16, slot), BF),
        pltpu.VMEM((count * 16, half), BF),
        pltpu.VMEM((count * 16, half), BF),
        pltpu.VMEM((count * 16, half), BF),
        pltpu.VMEM((width, 128), BF),
        pltpu.VMEM((nd, share, 128), BF),
        pltpu.VMEM((32, 128), BF),
        pltpu.VMEM((nd, 32, 128), BF),
        dma((5 + 2 * blocks,)),
        dma((chunks,)),
        dma((chunks,)),
        dma((chunks, 8)),
        dma((chunks, 8)),
        dma((count // 2,)),
        dma((count // 2,)),
        dma((count // 2,)),
        dma((count // 2,)),
        dma((count // 2,)),
        dma((2 * chips,)),
        dma((2 * chips,)),
        dma,
        dma,
        dma((nd,)),
        dma((nd,)),
        dma((nd,)),
        dma((nd,)),
        dma((2,)),
        dma((2,)),
        dma,
        dma,
        pltpu.VMEM((8, unit), F32),
        pltpu.VMEM((8, unit), F32),
    ]
    made = pl.pallas_call(
        functools.partial(tower, nd, nd * q_rows),
        out_shape=[o[0] for o in outs],
        in_specs=in_specs,
        out_specs=[o[1] for o in outs],
        scratch_shapes=scratch,
        compiler_params=pltpu.CompilerParams(
            collective_id=0, has_side_effects=True, vmem_limit_bytes=60 * MIB
        ),
        name="tower",
    )(
        lengths,
        tokens,
        queries,
        places.reshape(1, q_pad),
        w_qkv,
        b_qv,
        w_out,
        b_out.reshape(1, width),
        gain_one.reshape(1, width),
        shift_one.reshape(1, width),
        w_in,
        b_in.reshape(blocks, unit),
        w_back,
        b_back.reshape(1, width),
        gain_two.reshape(1, width),
    )
    sums, sums_in, loss, q_grad = made[14:18]
    g_outs = [
        (shape((rows, half), BF), hbm),
        (shape((rows, half), F32), vmem),
        (shape((3, share, half), F32), vmem),
        (shape((half, share), F32), vmem),
        (shape((share, units), F32), vmem),
        (shape((units, share), F32), vmem),
        (shape((16, width), F32), vmem),
    ]
    grads = pl.pallas_call(
        functools.partial(gradients, nd),
        out_shape=[o[0] for o in g_outs],
        in_specs=[hbm] + [vmem] * 16,
        out_specs=[o[1] for o in g_outs],
        scratch_shapes=[
            dma,
            pltpu.VMEM((count, half), F32),
            pltpu.VMEM((nd * count * 8, width), BF),
        ],
        compiler_params=pltpu.CompilerParams(vmem_limit_bytes=48 * MIB),
        name="gradients",
    )(*made[:17])
    activations, input_grad, grad_qkv, grad_out, grad_in, grad_back, small = grads

    def own_part(row, size):
        return lax.dynamic_slice(small, (row, dp * size), (1, size))[0]

    bias_share = half // nd
    grad_bias_qv = jnp.stack([own_part(8, bias_share), own_part(5, bias_share)])
    in_share = units // nd
    grad_bias_in = lax.dynamic_slice(sums_in[:blocks].reshape(units), (dp * in_share,), (in_share,))
    query_loss = lax.dynamic_slice(loss[0], (dp * 16,), (q_rows,))
    return (
        activations,
        query_loss,
        input_grad,
        q_grad[:q_rows],
        grad_qkv,
        grad_bias_qv,
        grad_out,
        own_part(4, share),
        own_part(2, share),
        own_part(3, share),
        grad_in,
        grad_bias_in,
        grad_back,
        own_part(1, share),
        own_part(0, share),
    )


def layer_norm(rows, gain, shift):
    center = jnp.mean(rows, axis=-1, keepdims=True)
    spread = rows - center
    second = jnp.mean(spread * spread, axis=-1, keepdims=True)
    return spread * lax.rsqrt(second + EPS) * gain + shift


def scaled_norm(rows, gain):
    center = jnp.mean(rows, axis=-1, keepdims=True)
    spread = rows - center
    second = jnp.mean(spread * spread, axis=-1, keepdims=True)
    return spread * lax.rsqrt(second + EPS) * gain


def gelu_exact(values):
    return jax.nn.gelu(values, approximate=False)


def first_rows(values, count):
    return values.reshape((count, values.shape[0] // count) + values.shape[1:])[:, 0]


def by_collectives(
    tokens,
    lengths,
    queries,
    positives,
    w_qkv,
    b_qv,
    w_out,
    b_out,
    gain_one,
    shift_one,
    w_in,
    b_in,
    w_back,
    b_back,
    gain_two,
):
    rows, width = tokens.shape
    count = lengths.shape[0]
    slot = rows // count
    local = w_qkv.shape[2]
    heads_here = local // HEAD
    scale = 1.0 / math.sqrt(HEAD)
    projected = jnp.einsum("rd,jdc->jrc", tokens, w_qkv, preferred_element_type=F32)
    bias_qv = b_qv.astype(F32)
    query = (projected[0] + bias_qv[0]).astype(BF)
    keyed = projected[1].astype(BF)
    value = (projected[2] + bias_qv[1]).astype(BF)
    block = min(count, max(1, 512 // slot))
    blocks = count // block
    valid = lax.broadcasted_iota(jnp.int32, (count, slot), 1) < lengths[:, None]
    split_shape = (blocks, block, slot, heads_here, HEAD)

    def attend(inputs):
        query_part, keyed_part, value_part, valid_part = inputs
        scores = (
            jnp.einsum(
                "pqhd,pkhd->phqk", query_part, keyed_part, preferred_element_type=F32
            )
            * scale
        )
        scores = jnp.where(valid_part[:, None, None, :], scores, MASKED)
        top = jnp.max(scores, axis=-1, keepdims=True)
        raised = jnp.exp(scores - top)
        total = jnp.sum(raised, axis=-1, keepdims=True)
        chance_low = (raised / total).astype(BF)
        mixed = jnp.einsum(
            "phqk,pkhd->pqhd", chance_low, value_part, preferred_element_type=F32
        )
        return (mixed.astype(BF), (top + jnp.log(total))[:, :, 0, 0])

    context, log_total = lax.map(
        attend,
        (
            query.reshape(split_shape),
            keyed.reshape(split_shape),
            value.reshape(split_shape),
            valid.reshape(blocks, block, slot),
        ),
    )
    context = context.reshape(rows, local)
    log_total = log_total.reshape(count, heads_here)
    partial_attn = jnp.dot(context, w_out, preferred_element_type=F32).astype(BF)
    attended = lax.psum(partial_attn, "mp").astype(F32) + b_out.astype(F32)
    resid_one = tokens.astype(F32) + attended
    gain_one_w = gain_one.astype(F32)
    shift_one_w = shift_one.astype(F32)
    gain_two_w = gain_two.astype(F32)
    norm_one = layer_norm(resid_one, gain_one_w, shift_one_w)
    norm_low = norm_one.astype(BF)
    inner = jnp.dot(norm_low, w_in, preferred_element_type=F32) + b_in.astype(F32)
    active = gelu_exact(inner).astype(BF)
    partial_ffn = jnp.dot(active, w_back, preferred_element_type=F32).astype(BF)
    resid_two = (
        norm_one + lax.psum(partial_ffn, "mp").astype(F32) + b_back.astype(F32)
    )
    output = scaled_norm(resid_two, gain_two_w)
    column = lax.axis_index("mp") * local
    activations = lax.dynamic_slice_in_dim(output, column, local, 1).astype(BF)
    cls_low = first_rows(output, count).astype(BF)
    query_rows = queries.shape[0]
    members = lax.axis_size("dp")
    query_total = query_rows * members
    own_query = lax.axis_index("dp") * query_rows
    gathered = lax.all_gather(cls_low, "dp", axis=0, tiled=True)
    similar = jnp.einsum("qd,pd->qp", queries, gathered, preferred_element_type=F32)
    mine = lax.dynamic_slice_in_dim(positives, own_query, query_rows)
    target = lax.broadcasted_iota(jnp.int32, similar.shape, 1) == mine[:, None]
    top = jnp.max(similar, axis=1, keepdims=True)
    log_sum = top[:, 0] + jnp.log(jnp.sum(jnp.exp(similar - top), axis=1))
    picked = jnp.sum(jnp.where(target, similar, 0.0), axis=1)
    query_loss = log_sum - picked
    slopes = (jnp.exp(similar - log_sum[:, None]) - target.astype(F32)) / query_total
    query_grad = jnp.dot(slopes, gathered.astype(F32), precision=lax.Precision.HIGHEST)
    queries_wide = queries.astype(F32)
    cls_grad = lax.psum_scatter(
        jnp.einsum("qp,qd->pd", slopes, queries_wide, precision=lax.Precision.HIGHEST),
        "dp",
        scatter_dimension=0,
        tiled=True,
    )
    _, norm_two_pull = jax.vjp(scaled_norm, first_rows(resid_two, count), gain_two_w)
    d_resid_two, grad_gain_two = norm_two_pull(cls_grad)
    grad_bias_back = jnp.sum(d_resid_two, axis=0)
    ffn_low = d_resid_two.astype(BF)
    grad_back = jnp.einsum(
        "pf,pd->fd", first_rows(active, count), ffn_low, preferred_element_type=F32
    )
    d_active = jnp.einsum("pd,fd->pf", ffn_low, w_back, preferred_element_type=F32)
    _, gelu_pull = jax.vjp(gelu_exact, first_rows(inner, count))
    d_inner = gelu_pull(d_active)[0]
    grad_bias_in = jnp.sum(d_inner, axis=0)
    inner_low = d_inner.astype(BF)
    grad_in = jnp.einsum(
        "pd,pf->df", first_rows(norm_low, count), inner_low, preferred_element_type=F32
    )
    back_norm = jnp.einsum("pf,df->pd", inner_low, w_in, preferred_element_type=F32)
    d_norm_one = d_resid_two + lax.psum(back_norm, "mp")
    _, norm_one_pull = jax.vjp(layer_norm, first_rows(resid_one, count), gain_one_w, shift_one_w)
    d_resid_one, grad_gain_one, grad_shift_one = norm_one_pull(d_norm_one)
    grad_bias_out = jnp.sum(d_resid_one, axis=0)
    attn_low = d_resid_one.astype(BF)
    grad_out = jnp.einsum(
        "pc,pd->cd", first_rows(context, count), attn_low, preferred_element_type=F32
    )
    d_context = jnp.einsum("pd,cd->pc", attn_low, w_out, preferred_element_type=F32).astype(
        BF
    )
    d_context = d_context.reshape(count, heads_here, HEAD)
    query_cls = first_rows(query, count).reshape(count, heads_here, HEAD)
    keyed_heads = keyed.reshape(count, slot, heads_here, HEAD)
    value_heads = value.reshape(count, slot, heads_here, HEAD)
    scores_cls = (
        jnp.einsum("phd,pkhd->phk", query_cls, keyed_heads, preferred_element_type=F32)
        * scale
    )
    scores_cls = jnp.where(valid[:, None, :], scores_cls, MASKED)
    chance = jnp.exp(scores_cls - log_total[:, :, None])
    d_chance = jnp.einsum(
        "phd,pkhd->phk", d_context, value_heads, preferred_element_type=F32
    )
    d_value = jnp.einsum(
        "phk,phd->pkhd", chance.astype(BF), d_context, preferred_element_type=F32
    )
    d_scores = chance * (d_chance - jnp.sum(chance * d_chance, axis=-1, keepdims=True))
    scores_low = d_scores.astype(BF)
    d_query = (
        jnp.einsum("phk,pkhd->phd", scores_low, keyed_heads, preferred_element_type=F32)
        * scale
    )
    d_keyed = (
        jnp.einsum("phk,phd->pkhd", scores_low, query_cls, preferred_element_type=F32)
        * scale
    )
    d_query = d_query.reshape(count, local)
    d_value = d_value.reshape(rows, local)
    query_low = d_query.astype(BF)
    keyed_value_low = jnp.stack(
        [d_keyed.reshape(rows, local).astype(BF), d_value.astype(BF)]
    )
    grad_bias_qv = jnp.stack([jnp.sum(d_query, axis=0), jnp.sum(d_value, axis=0)])
    grad_query_w = jnp.einsum(
        "pd,pc->dc", first_rows(tokens, count), query_low, preferred_element_type=F32
    )
    grad_kv = jnp.einsum("rd,jrc->jdc", tokens, keyed_value_low, preferred_element_type=F32)
    grad_qkv = jnp.concatenate([grad_query_w[None], grad_kv], axis=0)
    own_half = lax.dynamic_slice_in_dim(d_resid_one, column, local, 1)
    back_kv = jnp.einsum(
        "jrc,jdc->rd", keyed_value_low, w_qkv[1:], preferred_element_type=F32
    )
    back_query = jnp.einsum("pc,dc->pd", query_low, w_qkv[0], preferred_element_type=F32)
    back_all = back_kv.reshape(count, slot, width).at[:, 0].add(back_query).reshape(rows, width)
    input_grad = lax.psum_scatter(
        back_all.astype(BF), "mp", scatter_dimension=1, tiled=True
    ).astype(F32)
    input_grad = input_grad.reshape(count, slot, local).at[:, 0].add(own_half).reshape(rows, local)
    summed = (
        lax.psum_scatter(grad_qkv, "dp", scatter_dimension=1, tiled=True),
        lax.psum_scatter(grad_bias_qv, "dp", scatter_dimension=1, tiled=True),
        lax.psum_scatter(grad_out, "dp", scatter_dimension=1, tiled=True),
        lax.psum_scatter(grad_bias_out, "dp", scatter_dimension=0, tiled=True),
        lax.psum_scatter(grad_gain_one, "dp", scatter_dimension=0, tiled=True),
        lax.psum_scatter(grad_shift_one, "dp", scatter_dimension=0, tiled=True),
        lax.psum_scatter(grad_in, "dp", scatter_dimension=0, tiled=True),
        lax.psum_scatter(grad_bias_in, "dp", scatter_dimension=0, tiled=True),
        lax.psum_scatter(grad_back, "dp", scatter_dimension=1, tiled=True),
        lax.psum_scatter(grad_bias_back, "dp", scatter_dimension=0, tiled=True),
        lax.psum_scatter(grad_gain_two, "dp", scatter_dimension=0, tiled=True),
    )
    return (
        activations,
        query_loss,
        input_grad,
        query_grad,
        summed[0],
        summed[1],
        summed[2],
        summed[3],
        summed[4],
        summed[5],
        summed[6],
        summed[7],
        summed[8],
        summed[9],
        summed[10],
    )


def solution(mesh):
    in_specs = (
        P("dp", None),
        P("dp"),
        P("dp", None),
        P(),
        P(None, None, "mp"),
        P(None, "mp"),
        P("mp", None),
        P(),
        P(),
        P(),
        P(None, "mp"),
        P("mp"),
        P("mp", None),
        P(),
        P(),
    )
    out_specs = (
        P("dp", "mp"),
        P("dp"),
        P("dp", "mp"),
        P("dp", None),
        P(None, "dp", "mp"),
        P(None, ("mp", "dp")),
        P("mp", "dp"),
        P("dp"),
        P("dp"),
        P("dp"),
        P("dp", "mp"),
        P(("mp", "dp")),
        P("mp", "dp"),
        P("dp"),
        P("dp"),
    )
    groups = mesh.shape["dp"]
    fits = groups <= 16 and mesh.shape["mp"] == 2
    return jax.shard_map(
        functools.partial(per_device, groups) if fits else by_collectives,
        mesh=mesh,
        in_specs=in_specs,
        out_specs=out_specs,
        check_vma=False,
    )
```

time: 838 us -> 122 us (0.15)
  waiting for transfers between devices: 470 us -> 0 us
  matrix products: 99.2 us -> 0 us
  Pallas kernels: 0 us -> 89.9 us
  blocking collectives: 88.9 us -> 0 us
  local copies, waits for them, and re-layouts: 106 us -> 29.5 us
  other arithmetic: 49.6 us -> 0.57 us
  between operations: 17 us -> 0.71 us
    reduce_scatter x4 -> x0, waiting for transfers between devices: 264 us -> none  [the longest x1 79.6 us: per_device(): lax.psum_scatter(grad_in, 'dp', scatter_dimension=0, tiled=True)]
    psum x2 -> x0, waiting for transfers between devices: 149 us -> none  [the longest x1 87.9 us: per_device(): lax.psum(partial_attn, 'mp').astype(jnp.float32) + b_out.astype(jnp.float32)]
    dot_general x28 -> x0, matrix products: 99.2 us -> none  [the longest x1 32.5 us: per_device(): jnp.dot(norm_low, w_in, preferred_element_type=jnp.float32)]
    pallas_call x0 -> x2, Pallas kernels: none -> 89.9 us  [the longest x1 84.7 us: per_device(): pl.pallas_call(functools.partial(tower, nd, nd * q_rows), out_shape=[o[0]...]
    unnamed x1 -> x0, blocking collectives: 58.6 us -> none
    unnamed x10 -> x0, waiting for transfers between devices: 57 us -> none
    all_gather x1 -> x0, blocking collectives: 21.9 us -> none  [per_device(): gathered = lax.all_gather(cls_low, 'dp', axis=0, tiled=True)]
    reduce_sum x20 -> x0, other arithmetic: 21.2 us -> none  [the longest x2 5.99 us: scaled_norm(): center = jnp.mean(rows, axis=-1, keepdims=True)]
  transfers between devices with their start and end apart: 8 -> 0, of which waited for: 8 -> 0; matrix products, arithmetic and copies ran while one was open for 9% -> 0% of each run, Pallas kernels for 0% -> 0%
where the time goes in v1:
time: 122 us; the launch traced here: 121 us
  Pallas kernels  89.9 us (74%)
  local copies, waits for them, and re-layouts  29.5 us (24%)
    pallas_call x1, Pallas kernels, per_device(): pl.pallas_call(functools.partial(tower, nd, nd * q_rows), out_shape=[o[0]...  84.7 us
    unnamed x41, local copies, waits for them, and re-layouts  17.9 us
    pallas_call x1, Pallas kernels, per_device(): pl.pallas_call(functools.partial(gradients, nd), out_shape=[o[0] for o in...  5.14 us

profile of v1, /device:TPU:0, one launch (start us, length us, event | category | flops | bytes accessed | tf_op | source)
XLA Modules:
  0.0 120.6 jit_solution(9668466850785639844)
XLA Ops:
  0.6 0.8 reshape.58
  1.4 0.6 reshape.59.positives
  2.1 1.3 %reshape.63.b_in = bf16[3,512]{1,0:T(4,128)(2,1)} reshape(bf16[1536]{0:T(1024)(128)(2,1)} %param.26) | data formatting | bytes 6144 | tf_op jit(solution)/shard_map/reshape | solution.py:1006
  3.4 1.3 %reshape.60.b_out = bf16[1,768]{1,0:T(2,128)(2,1)} reshape(bf16[768]{0:T(1024)(128)(2,1)} %param.22) | data formatting | bytes 3072 | tf_op jit(solution)/shard_map/reshape | solution.py:1002
  4.6 1.3 %reshape.61.gain_one = bf16[1,768]{1,0:T(2,128)(2,1)} reshape(bf16[768]{0:T(1024)(128)(2,1)} %param.23) | data formatting | bytes 3072 | tf_op jit(solution)/shard_map/reshape | solution.py:1003
  5.9 1.3 %reshape.62.shift_one = bf16[1,768]{1,0:T(2,128)(2,1)} reshape(bf16[768]{0:T(1024)(128)(2,1)} %param.24) | data formatting | bytes 3072 | tf_op jit(solution)/shard_map/reshape | solution.py:1004
  7.1 1.3 %reshape.64.b_back = bf16[1,768]{1,0:T(2,128)(2,1)} reshape(bf16[768]{0:T(1024)(128)(2,1)} %param.28) | data formatting | bytes 3072 | tf_op jit(solution)/shard_map/reshape | solution.py:1008
  8.4 1.3 %reshape.65.gain_two = bf16[1,768]{1,0:T(2,128)(2,1)} reshape(bf16[768]{0:T(1024)(128)(2,1)} %param.29) | data formatting | bytes 3072 | tf_op jit(solution)/shard_map/reshape | solution.py:1009
  9.7 84.7 %tower.1 = (bf16[2048,384]{1,0:T(8,128)(2,1)}, bf16[2,128,256]{2,1,0:T(8,128)(2,1)}, bf16[2,128,384]{2,1,0:T(8,128)(2,1)}, bf16[16,48,128]{2,1,0:T(8,128)(2,1)},...) custom-call(s32[8]{0:T(128)} %lengths.1, ...), custom_call_target="tpu_custom_call" | custom-call | tf_op jit(solution)/shard_map/tower/pallas_call | solution.py:984
  94.4 0.0 copy-start
  94.4 1.4 %copy-done = bf16[2048,384]{1,0:T(8,128)(2,1)S(1)} copy-done((bf16[2048,384]{1,0:T(8,128)(2,1)S(1)}, bf16[2048,384]{1,0:T(8,128)(2,1)}, u32[]{:S(2)}) %copy-start) | copy-done | bytes 1572888
  95.8 0.0 copy-start.1
  95.8 1.0 copy-done.1
  96.8 0.0 copy-start.2
  96.8 1.0 copy-done.2
  97.8 0.0 copy-start.3
  97.8 0.9 copy-done.3
  98.7 0.0 copy-start.4
  98.7 0.9 copy-done.4
  99.7 0.0 copy-start.5
  99.7 0.9 copy-done.5
  100.6 0.0 copy-start.6
  100.6 0.9 copy-done.6
  101.5 0.0 copy-start.7
  101.5 0.9 copy-done.7
  102.4 0.0 copy-start.8
  102.4 0.9 copy-done.8
  103.4 0.0 copy-start.9
  103.4 0.9 copy-done.9
  104.3 0.0 copy-start.10
  104.3 0.9 copy-done.10
  105.2 0.0 copy-start.11
  105.2 0.9 copy-done.11
  106.1 0.0 copy-start.12
  106.1 0.9 copy-done.12
  107.0 0.0 copy-start.13
  107.0 0.9 copy-done.13
  107.9 0.0 copy-start.14
  107.9 0.7 copy-done.14
  108.6 0.0 copy-start.16
  108.6 0.7 copy-done.16
  109.3 0.0 copy-start.17
  109.3 0.7 copy-done.17
  110.0 0.0 copy-start.15
  110.0 0.0 copy-start.18
  110.0 5.1 %gradients.1 = (bf16[2048,384]{1,0:T(8,128)(2,1)}, f32[2048,384]{1,0:T(8,128)}, f32[3,48,384]{2,1,0:T(8,128)}, f32[384,48]{1,0:T(8,128)S(1)}, f32[48,1536]{1,0:T...) custom-call(bf16[2048,384]{1,0:T(8,128)(2,1)S(1)} %copy-done, bf16[2,128,256]{2,1,0:T(8,128)(2,1)S(1)} %copy-done.9, ...), custom_call_target="tpu_custom_call" | custom-call | tf_op jit(solution)/shard_map/gradients/pallas_call | solution.py:1021
  115.2 1.0 copy.31
  116.1 0.7 copy.30
  116.9 0.1 constant_dynamic-slice_fusion.1
  117.0 0.6 pad_maximum_fusion
  117.5 0.6 dynamic-slice_bitcast_fusion
  118.1 0.0 copy-done.15
  118.1 0.6 dynamic_slice.36
  118.7 0.7 slice.9
  119.4 0.6 dynamic-slice_bitcast_fusion.5
  120.0 0.0 copy-done.18
  120.0 0.6 copy.33
  (3 shorter events, 0.0 us)
Async XLA Ops:
  94.4 1.4 %copy-start = (bf16[2048,384]{1,0:T(8,128)(2,1)S(1)}, bf16[2048,384]{1,0:T(8,128)(2,1)}, u32[]{:S(2)}) copy-start(bf16[2048,384]{1,0:T(8,128)(2,1)} %get-tuple-element.40.act_in) | copy-start | bytes 4718596
  95.8 1.0 copy-start.1
  96.8 1.0 copy-start.2
  97.8 0.9 copy-start.3
  98.7 0.9 copy-start.4
  99.7 0.9 copy-start.5
  100.6 0.9 copy-start.6
  101.5 0.9 copy-start.7
  102.4 0.9 copy-start.8
  103.4 0.9 copy-start.9
  104.3 0.9 copy-start.10
  105.2 0.9 copy-start.11
  106.1 0.9 copy-start.12
  107.0 0.9 copy-start.13
  107.9 0.7 copy-start.14
  108.6 0.7 copy-start.16
  109.3 0.7 copy-start.17
  110.0 8.1 %copy-start.15 = (f32[8,512]{1,0:T(8,128)S(1)}, f32[8,512]{1,0:T(8,128)}, u32[]{:S(2)}) copy-start(f32[8,512]{1,0:T(8,128)} %get-tuple-element.55.sums_in) | copy-start | bytes 49156
  110.0 10.0 %copy-start.18 = (f32[16,768]{1,0:T(8,128)S(1)}, f32[16,768]{1,0:T(8,128)}, u32[]{:S(2)}) copy-start(f32[16,768]{1,0:T(8,128)} %get-tuple-element.59) | copy-start | bytes 147460

commit v2 on v1

--- a/solution.py
+++ b/solution.py
@@ -36,6 +36,20 @@
 def gelu_slope(h):
     bell = jnp.exp(-0.5 * h * h) * (1.0 / math.sqrt(2.0 * math.pi))
     return 0.5 * (1.0 + lax.erf(h * math.sqrt(0.5))) + h * bell
+
+
+def row_of(vector):
+    return vector[None, :].astype(F32)
+
+
+def exact(a, b):
+    return jnp.dot(a, b, preferred_element_type=F32, precision=lax.Precision.HIGHEST)
+
+
+def one_hot(shape, shift, dtype=F32):
+    row = lax.broadcasted_iota(jnp.int32, shape, 0)
+    column = lax.broadcasted_iota(jnp.int32, shape, 1)
+    return (row == column + shift).astype(dtype)
 
 
 def standard(rows):
@@ -316,7 +330,8 @@
         copy.wait()
     pl.semaphore_wait(barrier, 2 * nd - 1)
     bin_own[...] = jnp.zeros_like(bin_own)
-    bin_own[0:blocks, :] = b_in[...].astype(F32)
+    for u in range(blocks):
+        bin_own[u : u + 1, :] = row_of(b_in[pl.ds(u * unit, unit)])
     bias_copy = remote(bin_own, bin_far, b_send, b_recv, pair)
     bias_copy.start()
     for k in range(chunks):
@@ -448,11 +463,11 @@
     tick(2)
     tick(3)
     complete(0)
-    bo = b_out[0:1, :].astype(F32)
-    g1 = gain_one[0:1, :].astype(F32)
-    s1 = shift_one[0:1, :].astype(F32)
-    g2 = gain_two[0:1, :].astype(F32)
-    bb = b_back[0:1, :].astype(F32)
+    bo = row_of(b_out[...])
+    g1 = row_of(gain_one[...])
+    s1 = row_of(shift_one[...])
+    g2 = row_of(gain_two[...])
+    bb = row_of(b_back[...])
 
     def feed_own(i, carry):
         ctx_came(i).wait_recv()
@@ -568,7 +583,13 @@
     similar = nt(cls, q_all[...])
     top = jnp.max(similar, axis=0, keepdims=True)
     log_sum = top + jnp.log(jnp.sum(jnp.exp(similar - top), axis=0, keepdims=True))
-    target = lax.broadcasted_iota(jnp.int32, similar.shape, 0) == positives[0:1, :]
+    q_count = query_total // nd
+    from_q = lax.broadcasted_iota(jnp.int32, (query_total, q_pad), 0)
+    to_q = lax.broadcasted_iota(jnp.int32, (query_total, q_pad), 1)
+    spot = lax.div(from_q, q_count) * 16 + lax.rem(from_q, q_count)
+    wanted = jnp.broadcast_to(row_of(positives[...]), (8, query_total)) + 1.0
+    place = exact(wanted, (spot == to_q).astype(F32))[0:1, :] - 1.0
+    target = lax.broadcasted_iota(jnp.int32, similar.shape, 0).astype(F32) == place
     picked = jnp.sum(jnp.where(target, similar, 0.0), axis=0, keepdims=True)
     o_loss[...] = jnp.broadcast_to(log_sum - picked, o_loss.shape)
     slopes = (jnp.exp(similar - log_sum) - target.astype(F32)) * (1.0 / query_total)
@@ -748,6 +769,38 @@
 def gradients(
     nd,
     act_in,
+    coef_in,
+    rank_in,
+    factor_in,
+    dquery_in,
+    active_in,
+    inner_in,
+    context_in,
+    qcls_in,
+    dctx_in,
+    norm_in,
+    ffn_in,
+    attn_in,
+    tok_in,
+    sums_in,
+    sums_units_in,
+    loss_in,
+    qgrad_in,
+    act_out,
+    query_loss,
+    input_grad,
+    query_grad,
+    grad_qkv,
+    grad_bias_qv,
+    grad_out,
+    grad_bias_out,
+    grad_gain_one,
+    grad_shift_one,
+    grad_in,
+    grad_bias_in,
+    grad_back,
+    grad_bias_back,
+    grad_gain_two,
     coef,
     rank,
     factor,
@@ -762,53 +815,67 @@
     attn,
     tok,
     sums,
-    sums_in,
+    sums_units,
     loss,
-    act_out,
-    input_grad,
-    grad_qkv,
-    grad_out,
-    grad_in,
-    grad_back,
-    small,
+    qgrad,
+    sems,
     act_sem,
-    wide,
+    act_buf,
+    in_buf,
+    in_sems,
     rhs,
 ):
     dp = lax.axis_index("dp")
-    mp = lax.axis_index("mp")
-    copy = pltpu.make_async_copy(act_in, act_out, act_sem)
-    copy.start()
+    act_load = pltpu.make_async_copy(act_in, act_buf, act_sem.at[0])
+    act_store = pltpu.make_async_copy(act_buf, act_out, act_sem.at[1])
+    act_load.start()
+    pairs = (
+        (coef_in, coef),
+        (rank_in, rank),
+        (factor_in, factor),
+        (dquery_in, dquery),
+        (qcls_in, qcls),
+        (dctx_in, dctx),
+        (active_in, active),
+        (inner_in, inner),
+        (context_in, context),
+        (norm_in, norm),
+        (ffn_in, ffn),
+        (attn_in, attn),
+        (tok_in, tok),
+        (sums_in, sums),
+        (sums_units_in, sums_units),
+        (loss_in, loss),
+        (qgrad_in, qgrad),
+    )
+    loads = [pltpu.make_async_copy(src, dst, sems.at[i]) for i, (src, dst) in enumerate(pairs)]
+    for load in loads:
+        load.start()
     passages, width = ffn.shape
     half = width // 2
-    heads = half // HEAD
     share = width // nd
     count = passages // nd
     slot = coef.shape[2]
+    for load in loads[:2]:
+        load.wait()
+
+    def input_copy(p):
+        at = pl.ds(mult(p * slot, slot), slot)
+        return pltpu.make_async_copy(in_buf.at[at, :], input_grad.at[at, :], in_sems.at[p])
 
     def input_rows(p, carry):
         rows16 = pl.ds(mult(p * 16, 16), 16)
-        at = pl.ds(mult(p * slot, slot), slot)
         both = jnp.concatenate([coef[0, rows16, :], coef[1, rows16, :]], axis=0)
         right = jnp.concatenate([rank[0, rows16, :], rank[1, rows16, :]], axis=0)
-        input_grad[at, :] = tn(both, right)
+        in_buf[pl.ds(mult(p * slot, slot), slot), :] = tn(both, right)
+        input_copy(p).start()
         return carry
 
     lax.fori_loop(0, count, input_rows, 0)
-
-    own = lax.broadcasted_iota(jnp.int32, (width, share), 0)
-    pick = (own == lax.broadcasted_iota(jnp.int32, (width, share), 1) + dp * share).astype(BF)
-    own_t = lax.broadcasted_iota(jnp.int32, (share, width), 1)
-    pick_t = (own_t == lax.broadcasted_iota(jnp.int32, (share, width), 0) + dp * share).astype(BF)
-    ffn_own = nn(ffn[...], pick).astype(BF)
-    attn_own = nn(attn[...], pick).astype(BF)
-    norm_own = nt(pick_t, norm[...]).astype(BF)
-    tok_own = nt(pick_t, tok[...]).astype(BF)
-    grad_out[...] = tn(context[...], attn_own)
-    unit = active.shape[2]
-    for u in range(active.shape[0]):
-        grad_back[u * unit : (u + 1) * unit, :] = tn(active[u], ffn_own)
-        grad_in[:, u * unit : (u + 1) * unit] = nn(norm_own, inner[u])
+    act_load.wait()
+    act_store.start()
+    for load in loads[2:]:
+        load.wait()
 
     spread = lax.broadcasted_iota(jnp.int32, (8, half), 0) == lax.div(
         lax.broadcasted_iota(jnp.int32, (8, half), 1), HEAD
@@ -816,20 +883,16 @@
     fkind = count * 8
 
     def build(s, carry):
-        wide[...] = qcls[pl.ds(mult(s * count, 8), count), :].astype(F32) * 0.125
-        d_rows = dctx[pl.ds(mult(s * count, 8), count), :].astype(F32)
-        q_rows = wide[...]
-        k_blocks = [
-            jnp.where(spread, q_rows[p : p + 1, :], 0.0) for p in range(count)
-        ]
-        v_blocks = [
-            jnp.where(spread, d_rows[p : p + 1, :], 0.0) for p in range(count)
-        ]
-        rhs[pl.ds(mult(s * fkind, 16), fkind), 0:half] = jnp.concatenate(k_blocks, 0).astype(BF)
-        rhs[pl.ds(mult(s * fkind, 16), fkind), half:] = jnp.concatenate(v_blocks, 0).astype(BF)
+        d_rows = dctx[pl.ds(mult(s * 2 * count, 16), 2 * count), :].astype(F32)
+        q_rows = qcls[pl.ds(mult(s * 2 * count, 16), 2 * count), :].astype(F32) * 0.125
+        k_blocks = [jnp.where(spread, q_rows[p : p + 1, :], 0.0) for p in range(2 * count)]
+        v_blocks = [jnp.where(spread, d_rows[p : p + 1, :], 0.0) for p in range(2 * count)]
+        here = pl.ds(mult(s * 2 * fkind, 16), 2 * fkind)
+        rhs[here, 0:half] = jnp.concatenate(k_blocks, 0).astype(BF)
+        rhs[here, half:] = jnp.concatenate(v_blocks, 0).astype(BF)
         return carry
 
-    lax.fori_loop(0, nd, build, 0)
+    lax.fori_loop(0, nd // 2, build, 0)
     grad_k = jnp.zeros((share, half), F32)
     grad_v = jnp.zeros((share, half), F32)
     for s in range(0, nd, 4):
@@ -839,17 +902,57 @@
         grad_v = grad_v + nn(left_v, rhs[s * fkind : (s + 4) * fkind, half:])
     grad_qkv[1] = grad_k
     grad_qkv[2] = grad_v
+
+    pick = one_hot((width, share), dp * share)
+    pick_low = pick.astype(BF)
+    row = lax.broadcasted_iota(jnp.int32, (share, width), 0)
+    column = lax.broadcasted_iota(jnp.int32, (share, width), 1)
+    pick_t = (column == row + dp * share).astype(BF)
+    ffn_own = nt(pick_t, ffn[...]).astype(BF)
+    attn_own = nt(pick_t, attn[...]).astype(BF)
+    norm_own = nt(pick_t, norm[...]).astype(BF)
+    tok_own = nt(pick_t, tok[...]).astype(BF)
+    grad_out[...] = nn(attn_own, context[...])
+    unit = active.shape[2]
+    blocks = active.shape[0]
+    for u in range(blocks):
+        cols = slice(u * unit, (u + 1) * unit)
+        grad_back[:, cols] = nn(ffn_own, active[u])
+        grad_in[:, cols] = nn(norm_own, inner[u])
     dq_sum = []
-    grad_q = []
     for b in range(half // 128):
-        cols = dquery[:, pl.ds(0, 32), :].astype(F32)[:, b * 8 : b * 8 + 8, :]
-        cols = cols.reshape(passages, 128)
+        cols = dquery[...].astype(F32)[:, b * 8 : b * 8 + 8, :].reshape(passages, 128)
         dq_sum.append(jnp.sum(cols, axis=0, keepdims=True))
         grad_qkv[0, :, b * 128 : b * 128 + 128] = nn(tok_own, cols.astype(BF))
-    small[0:8, :] = sums[...]
-    small[8:9, 0:half] = jnp.concatenate(dq_sum, axis=1)
-    small[9:16, :] = jnp.zeros((7, width), F32)
-    copy.wait()
+
+    mine = exact(sums[...], pick)
+    grad_gain_two[...] = mine[0:1, :].reshape(share)
+    grad_bias_back[...] = mine[1:2, :].reshape(share)
+    grad_gain_one[...] = mine[2:3, :].reshape(share)
+    grad_shift_one[...] = mine[3:4, :].reshape(share)
+    grad_bias_out[...] = mine[4:5, :].reshape(share)
+    part = half // nd
+    both = jnp.concatenate([jnp.concatenate(dq_sum, axis=1), sums[5:6, 0:half]], axis=0)
+    wide = jnp.concatenate([both, jnp.zeros((6, half), F32)], axis=0)
+    grad_bias_qv[...] = exact(wide, one_hot((half, part), dp * part))[0:2, :]
+    in_share = grad_bias_in.shape[0]
+    total = jnp.zeros((8, in_share), F32)
+    for u in range(blocks):
+        total = total + exact(
+            jnp.broadcast_to(sums_units[u : u + 1, :], (8, unit)),
+            one_hot((unit, in_share), dp * in_share - u * unit),
+        )
+    grad_bias_in[...] = total[0:1, :].reshape(in_share)
+    q_rows = query_loss.shape[0]
+    query_loss[...] = exact(loss[...], one_hot((loss.shape[1], q_rows), dp * 16))[0:1, :].reshape(q_rows)
+    query_grad[...] = qgrad[0:q_rows, :]
+
+    def input_wait(p, carry):
+        input_copy(p).wait()
+        return carry
+
+    lax.fori_loop(0, count, input_wait, 0)
+    act_store.wait()
 
 
 def per_device(nd, *arrays):
@@ -884,10 +987,6 @@
     q_rows = queries.shape[0]
     q_pad = nd * 16
     share = width // nd
-    dp = lax.axis_index("dp")
-    mp = lax.axis_index("mp")
-
-    places = jnp.pad(positives.reshape(nd, q_rows), ((0, 0), (0, 16 - q_rows)), constant_values=-1)
     vmem = pl.BlockSpec(memory_space=pltpu.VMEM)
     hbm = pl.BlockSpec(memory_space=pl.ANY)
     smem = pl.BlockSpec(memory_space=pltpu.SMEM)
@@ -995,69 +1094,57 @@
         lengths,
         tokens,
         queries,
-        places.reshape(1, q_pad),
+        positives,
         w_qkv,
         b_qv,
         w_out,
-        b_out.reshape(1, width),
-        gain_one.reshape(1, width),
-        shift_one.reshape(1, width),
+        b_out,
+        gain_one,
+        shift_one,
         w_in,
-        b_in.reshape(blocks, unit),
+        b_in,
         w_back,
-        b_back.reshape(1, width),
-        gain_two.reshape(1, width),
-    )
-    sums, sums_in, loss, q_grad = made[14:18]
+        b_back,
+        gain_two,
+    )
     g_outs = [
         (shape((rows, half), BF), hbm),
-        (shape((rows, half), F32), vmem),
+        (shape((q_rows,), F32), vmem),
+        (shape((rows, half), F32), hbm),
+        (shape((q_rows, width), F32), vmem),
         (shape((3, share, half), F32), vmem),
-        (shape((half, share), F32), vmem),
+        (shape((2, half // nd), F32), vmem),
+        (shape((share, half), F32), vmem),
+        (shape((share,), F32), vmem),
+        (shape((share,), F32), vmem),
+        (shape((share,), F32), vmem),
         (shape((share, units), F32), vmem),
-        (shape((units, share), F32), vmem),
-        (shape((16, width), F32), vmem),
+        (shape((units // nd,), F32), vmem),
+        (shape((share, units), F32), vmem),
+        (shape((share,), F32), vmem),
+        (shape((share,), F32), vmem),
     ]
     grads = pl.pallas_call(
         functools.partial(gradients, nd),
         out_shape=[o[0] for o in g_outs],
-        in_specs=[hbm] + [vmem] * 16,
+        in_specs=[hbm] * len(outs),
         out_specs=[o[1] for o in g_outs],
-        scratch_shapes=[
-            dma,
-            pltpu.VMEM((count, half), F32),
+        scratch_shapes=[pltpu.VMEM(o[0].shape, o[0].dtype) for o in outs[1:]]
+        + [
+            dma((len(outs) - 1,)),
+            dma((2,)),
+            pltpu.VMEM((rows, half), BF),
+            pltpu.VMEM((rows, half), F32),
+            dma((count,)),
             pltpu.VMEM((nd * count * 8, width), BF),
         ],
-        compiler_params=pltpu.CompilerParams(vmem_limit_bytes=48 * MIB),
+        compiler_params=pltpu.CompilerParams(vmem_limit_bytes=62 * MIB),
         name="gradients",
-    )(*made[:17])
-    activations, input_grad, grad_qkv, grad_out, grad_in, grad_back, small = grads
-
-    def own_part(row, size):
-        return lax.dynamic_slice(small, (row, dp * size), (1, size))[0]
-
-    bias_share = half // nd
-    grad_bias_qv = jnp.stack([own_part(8, bias_share), own_part(5, bias_share)])
-    in_share = units // nd
-    grad_bias_in = lax.dynamic_slice(sums_in[:blocks].reshape(units), (dp * in_share,), (in_share,))
-    query_loss = lax.dynamic_slice(loss[0], (dp * 16,), (q_rows,))
-    return (
-        activations,
-        query_loss,
-        input_grad,
-        q_grad[:q_rows],
-        grad_qkv,
-        grad_bias_qv,
-        grad_out,
-        own_part(4, share),
-        own_part(2, share),
-        own_part(3, share),
-        grad_in,
-        grad_bias_in,
-        grad_back,
-        own_part(1, share),
-        own_part(0, share),
-    )
+    )(*made)
+    grads = list(grads)
+    grads[6] = grads[6].T
+    grads[12] = grads[12].T
+    return tuple(grads)
 
 
 def layer_norm(rows, gain, shift):

time: 122 us -> 91.6 us (0.75)
  local copies, waits for them, and re-layouts: 29.5 us -> 0 us
    unnamed x41 -> x0, local copies, waits for them, and re-layouts: 17.9 us -> none
    reshape x9 -> x0, local copies, waits for them, and re-layouts: 9.01 us -> none  [the longest x1 1.29 us: per_device(): b_in.reshape(blocks, unit)]
    dynamic_slice x3 -> x0, local copies, waits for them, and re-layouts: 1.24 us -> none  [the longest x1 0.59 us: per_device(): lax.dynamic_slice(sums_in[:blocks].reshape(units), (dp * in_share,), (in_...]
where the time goes in v2:
time: 91.6 us; the launch traced here: 91.4 us
  Pallas kernels  90.8 us (99%)
    pallas_call x1, Pallas kernels, per_device(): pl.pallas_call(functools.partial(tower, nd, nd * q_rows), out_shape=[o[0]...  84.8 us
    pallas_call x1, Pallas kernels, per_device(): pl.pallas_call(functools.partial(gradients, nd), out_shape=[o[0] for o in...  5.99 us

profile of v2, /device:TPU:0, one launch (start us, length us, event | category | flops | bytes accessed | tf_op | source)
XLA Modules:
  0.0 91.4 jit_solution(9088125657257139375)
XLA Ops:
  0.7 84.8 %tower.1 = (bf16[2048,384]{1,0:T(8,128)(2,1)}, bf16[2,128,256]{2,1,0:T(8,128)(2,1)}, bf16[2,128,384]{2,1,0:T(8,128)(2,1)}, bf16[16,48,128]{2,1,0:T(8,128)(2,1)},...) custom-call(s32[8]{0:T(128)} %lengths.1, ...), custom_call_target="tpu_custom_call" | custom-call | tf_op jit(solution)/shard_map/tower/pallas_call | solution.py:1083
  85.4 6.0 %gradients.1 = (bf16[2048,384]{1,0:T(8,128)(2,1)}, f32[12]{0:T(128)}, f32[2048,384]{1,0:T(8,128)}, f32[12,768]{1,0:T(8,128)}, f32[3,48,384]{2,1,0:T(8,128)}, /*i...) custom-call(bf16[2048,384]{1,0:T(8,128)(2,1)} %get-tuple-element.48., ...), custom_call_target="tpu_custom_call" | custom-call | tf_op jit(solution)/shard_map/gradients/pallas_call | solution.py:1127

commit v3 on v2

--- a/solution.py
+++ b/solution.py
@@ -93,32 +93,31 @@
     b_back,
     gain_two,
     out_act,
-    o_coef,
-    o_rank,
-    o_factor,
-    o_dquery,
-    o_active,
-    o_inner,
-    o_context,
-    o_qcls,
-    o_dctx,
-    o_norm,
-    o_ffn,
-    o_attn,
-    o_tok,
-    o_sums,
-    o_sums_in,
-    o_loss,
-    o_qgrad,
+    h_coef,
+    h_rank,
+    h_factor,
+    h_active,
+    h_inner,
+    h_context,
+    h_qcls,
+    h_dctx,
+    h_norm,
+    h_ffn,
+    h_attn,
+    h_tok,
+    h_sums,
+    h_sums_in,
+    h_loss,
+    h_qgrad,
     tok,
     wq,
+    wq_far,
     wo,
     wi,
     wb,
     keyb,
     valb,
     ctx,
-    ctx_send,
     norm_low,
     acc,
     act_far,
@@ -148,16 +147,11 @@
     rank_send,
     rank_far,
     fac_send,
-    fac_all,
-    dq_send,
-    dq_all,
     loc_sem,
     ysend,
     yrecv,
     w_send,
     w_recv,
-    c_send,
-    c_recv,
     o_send,
     o_recv,
     o_loc,
@@ -167,14 +161,29 @@
     gs_recv,
     f_send,
     f_recv,
-    q_send,
-    q_recv,
     m_send,
     m_recv,
     b_send,
     b_recv,
     bin_own,
     bin_far,
+    out_sem,
+    o_coef,
+    o_rank,
+    o_factor,
+    o_active,
+    o_inner,
+    o_context,
+    o_qcls,
+    o_dctx,
+    o_norm,
+    o_ffn,
+    o_attn,
+    o_tok,
+    o_sums,
+    o_sums_in,
+    o_loss,
+    o_qgrad,
 ):
     dp = lax.axis_index("dp")
     mp = lax.axis_index("mp")
@@ -234,36 +243,49 @@
     for copy in loads:
         copy.start()
 
-    chunks = 1 + 2 * blocks
+    first_in = 4
+    first_back = 4 + blocks
+    chunks = 4 + 2 * blocks
+    direct = (3, chunks - 1)
 
     def piece(k, q, c, which, side=None):
-        if k == 0:
-            size = half // 8
-            at = mult(which * half + (c * 4 + q) * size, 16)
-            cols = pl.ds(0, width) if side is None else pl.ds(side * half, half)
-            return wo.at[pl.ds(at, size), cols]
-        if k <= blocks:
+        if k < 3 or first_in <= k < first_back:
             size = width // 8
-            at = (c * 4 + q) * size
+            at = (c * 4 if q is None else c * 4 + q) * size
+            size = 4 * size if q is None else size
             if side is not None:
                 size = size // 2
                 at = at + side * size
-            return wi.at[which, k - 1, pl.ds(mult(at, 16), size), :]
-        size = unit // 8
+            here = pl.ds(mult(at, 16), size)
+            return wq_far.at[here, pl.ds(k * half, half)] if k < 3 else wi.at[which, k - 4, here, :]
         cols = pl.ds(0, width) if side is None else pl.ds(side * half, half)
-        return wb.at[which, k - 1 - blocks, pl.ds(mult((c * 4 + q) * size, 16), size), cols]
+        if k == 3:
+            size = half // 2
+            return wo.at[pl.ds(mult(which * half + c * size, 16), size), cols]
+        whole = k in direct or q is None
+        size = unit // 2 if whole else unit // 8
+        at = c * size if whole else (c * 4 + q) * size
+        return wb.at[which, k - first_back, pl.ds(mult(at, 16), size), cols]
+
+    def sent_bytes(k):
+        if k < 3:
+            return wq_far.at[pl.ds(0, 7 * width // 8), pl.ds(k * half, half)]
+        if k == 3:
+            return piece(k, None, core, far)
+        if k < first_back:
+            return wi.at[far, k - 4, pl.ds(0, 7 * width // 8), :]
+        return wb.at[far, k - first_back, pl.ds(0, unit // 2 if k in direct else 7 * unit // 8), :]
 
     def source(k):
-        if k == 0:
-            size = half // 8
-            return w_out.at[pl.ds(mult((core * 4 + quarter) * size, 16), size), :]
-        if k <= blocks:
+        if k < 3 or first_in <= k < first_back:
             size = width // 8
-            at = mult((core * 4 + quarter) * size, 16)
-            return w_in.at[pl.ds(at, size), pl.ds((k - 1) * unit, unit)]
-        size = unit // 8
-        at = mult((k - 1 - blocks) * unit + (core * 4 + quarter) * size, 16)
-        return w_back.at[pl.ds(at, size), :]
+            here = pl.ds(mult((core * 4 + quarter) * size, 16), size)
+            return w_qkv.at[k, here, :] if k < 3 else w_in.at[here, pl.ds((k - 4) * unit, unit)]
+        if k == 3:
+            return w_out.at[pl.ds(mult(core * (half // 2), 16), half // 2), :]
+        size = unit // 2 if k in direct else unit // 8
+        at = core * size if k in direct else (core * 4 + quarter) * size
+        return w_back.at[pl.ds(mult((k - first_back) * unit + at, 16), size), :]
 
     def remote(src, dst, ss, rs, device):
         return pltpu.make_async_remote_copy(
@@ -282,60 +304,54 @@
 
     def send(k, lane, q, c, side, device):
         ref = piece(k, q, c, far, side)
-        return remote(ref, ref, w_send.at[k, lane], w_recv.at[k, lane], device)
+        return remote(ref, ref, w_send.at[k], w_recv.at[k, lane], device)
 
     def lane(k, n):
-        q = (quarter, quarter, quarter_z, quarter_x, quarter, quarter_x, quarter_z, quarter_d)[n]
-        side = (None, None, 0, 1, None, None, None, None)[n]
-        return send(k, n, q, core, side, (near_x, near_z, near_x, near_z)[n] if n < 4 else sibling)
+        q = (quarter, quarter, quarter_z, quarter_x, None)[n]
+        side = (None, None, 0, 1, None)[n]
+        return send(k, n, q, core, side, (near_x, near_z, near_x, near_z, sibling)[n])
 
     def arrival(k, n):
-        q = (quarter_x, quarter_z, quarter_d, quarter_d, quarter, quarter_x, quarter_z, quarter_d)[n]
-        side = (None, None, 0, 1, None, None, None, None)[n]
+        q = (quarter_x, quarter_z, quarter_d, quarter_d, None)[n]
+        side = (None, None, 0, 1, None)[n]
         c = core if n < 4 else 1 - core
-        return send(k, n, q, c, side, (near_x, near_z, near_x, near_z)[n] if n < 4 else sibling)
+        return send(k, n, q, c, side, (near_x, near_z, near_x, near_z, sibling)[n])
 
     def step_one(k):
         remote(
             source(k), piece(k, quarter, core, far), ysend.at[k], yrecv.at[k], pair
         ).wait_recv()
-        for n in (0, 1, 4):
+        for n in (4,) if k in direct else (0, 1):
             lane(k, n).start()
 
     def step_two(k):
         arrival(k, 1).wait_recv()
         lane(k, 2).start()
         arrival(k, 0).wait_recv()
-        for n in (3, 5, 6):
-            lane(k, n).start()
+        lane(k, 3).start()
 
     def step_three(k):
         arrival(k, 2).wait_recv()
         arrival(k, 3).wait_recv()
-        lane(k, 7).start()
+        lane(k, 4).start()
 
     def complete(k):
-        for n in range(4, 8):
-            arrival(k, n).wait_recv()
-
-    def tick(i):
-        if i < chunks:
-            step_one(i)
-        if 0 <= i - 1 < chunks:
-            step_two(i - 1)
-        if 0 <= i - 2 < chunks:
-            step_three(i - 2)
+        arrival(k, 4).wait_recv()
+
+    def spent(window, sem):
+        pltpu.make_async_copy(window, window, sem).wait()
+
+    def advance(*steps):
+        for stage_of, k in steps:
+            (step_one, step_two, step_three)[stage_of - 1](k)
 
     for copy in loads[:4]:
         copy.wait()
-    pl.semaphore_wait(barrier, 2 * nd - 1)
     bin_own[...] = jnp.zeros_like(bin_own)
     for u in range(blocks):
         bin_own[u : u + 1, :] = row_of(b_in[pl.ds(u * unit, unit)])
+    bin_own[6:8, 0:half] = b_qv[...].astype(F32)
     bias_copy = remote(bin_own, bin_far, b_send, b_recv, pair)
-    bias_copy.start()
-    for k in range(chunks):
-        cross(k).start()
 
     lane_pair = lax.broadcasted_iota(jnp.int32, (slot, 128), 1)
     key_place = lax.broadcasted_iota(jnp.int32, (1, slot), 1)
@@ -349,33 +365,7 @@
     row_place = lax.broadcasted_iota(jnp.int32, (8, slot), 0)
     first_key = (lax.broadcasted_iota(jnp.int32, (8, slot), 1) == 0).astype(F32)
 
-    def ctx_copy(i):
-        there = ctx.at[pl.ds(mult(i * slot, 16), slot), pl.ds(m_col, half)]
-        return remote(
-            ctx_send.at[pl.ds(mult(i * slot, 16), slot), :], there, c_send.at[i], c_recv.at[i], pair
-        )
-
-    def ctx_came(i):
-        here = ctx.at[pl.ds(mult(i * slot, 16), slot), pl.ds(f_col, half)]
-        return remote(
-            ctx_send.at[pl.ds(mult(i * slot, 16), slot), :], here, c_send.at[i], c_recv.at[i], pair
-        )
-
-    def attend(i, carry):
-        theirs = i < own
-        side = jnp.where(theirs, far, mp)
-        place = lax.rem(i, own)
-        p = side * own + place
-        at = mult(p * slot, slot)
-        x = tok[pl.ds(at, slot), :]
-        made = nn(x, wq[...])
-        query = ((made[:, :half] + bias_q).astype(BF).astype(F32) * 0.125).astype(BF)
-        keyed = made[:, half : 2 * half].astype(BF)
-        value = (made[:, 2 * half :] + bias_v).astype(BF)
-        keyb[pl.ds(at, slot), :] = keyed
-        valb[pl.ds(at, slot), :] = value
-        length = lengths[p]
-        bias = jnp.where(key_place < length, 0.0, MASKED)
+    def mix(query, keyed, value, bias):
         done = []
         for t in range(half // 128):
             q2 = query[:, 128 * t : 128 * t + 128]
@@ -389,40 +379,102 @@
                 o = nn(e, v2)
                 parts.append(o[:, :128] / o[:, 128:])
             done.append(jnp.where(lane_pair < HEAD, parts[0], parts[1]))
-        mixed = jnp.concatenate(done, axis=1)
-        low = mixed.astype(BF)
-        stage[pl.ds(p, 1), :] = mixed[0:1, :]
+        return jnp.concatenate(done, axis=1).astype(BF)
+
+    def first_row(p, x, query, keyed, value, bias):
         tcls[pl.ds(p, 1), :] = x[0:16, :].astype(F32)[0:1, :]
-        q_row = query[0:16, :].astype(F32)[0:1, :]
-        q_heads = jnp.where(head_mask, q_row, 0.0).astype(BF)
+        q_heads = jnp.where(head_mask, query.astype(F32)[0:1, :], 0.0).astype(BF)
         s = nt(q_heads, keyed) + bias
         e = jnp.exp(s - jnp.max(s, axis=1, keepdims=True))
         c = jnp.where(live, e / jnp.sum(e, axis=1, keepdims=True), 0.0)
         chance[p] = c
         c_low = c.astype(BF)
+        mixed = jnp.where(head_mask, nn(c_low, value), 0.0)
+        stage[pl.ds(p, 1), :] = jnp.sum(mixed, axis=0, keepdims=True)
         coef_own[pl.ds(mult(p * 16, 16), 8), :] = jnp.where(row_place == heads, first_key, c)
         factor[pl.ds(mult(p * 8, 8), 8), :] = nn(c_low, x)
 
-        @pl.when(theirs)
+    theirs_plan = (((1, 0),), (), ((1, 1),), ())
+    gap_plan = ((1, 2), (2, 0), (2, 1), (2, 2), (3, 0), (3, 1), (1, 3), (3, 2))
+    far_plan = ((), ((1, 4),), (), ((1, 5),))
+    feed_plan = ((), ((2, 4), (1, 7)), ((2, 5), (1, 8)), ((3, 4),))
+    feed_mid_plan = (((1, 6),), (), ((2, 6),), ((2, 7),))
+    in_plan = (
+        (((3, 5),), ()),
+        (((2, 8), (1, 9)), ((3, 6),)),
+        (((3, 7),), ((3, 8),)),
+    )
+
+    def move_on(i, plan):
+        for j, steps in enumerate(plan):
+            if steps:
+
+                @pl.when(i == j)
+                def _():
+                    advance(*steps)
+
+    def key_bias(p):
+        return jnp.where(key_place < lengths[p], 0.0, MASKED)
+
+    def attend_theirs(i, carry):
+        move_on(i, theirs_plan)
+        p = far * own + i
+        at = mult(p * slot, slot)
+        x = tok[pl.ds(at, slot), :]
+        made = nn(x, wq[:, half:])
+        keyed = made[:, :half].astype(BF)
+        value = (made[:, half:] + bias_v).astype(BF)
+        keyb[pl.ds(at, slot), :] = keyed
+        valb[pl.ds(at, slot), :] = value
+        query = ((nn(x[0:16, :], wq[:, :half]) + bias_q).astype(BF).astype(F32) * 0.125).astype(BF)
+        first_row(p, x, query, keyed, value, key_bias(p))
+        return carry
+
+    def attend_own(i, carry):
+        @pl.when(i == 1)
         def _():
-            ctx_send[pl.ds(mult(place * slot, 16), slot), :] = low
-            ctx_copy(place).start()
-
-        @pl.when(i >= own)
-        def _():
-            ctx[pl.ds(mult(place * slot, 16), slot), pl.ds(m_col, half)] = low
-
-        @pl.when(i == own)
-        def _():
-            tick(0)
-
-        @pl.when(i == own + 2)
-        def _():
-            tick(1)
-
+            pl.semaphore_wait(barrier, 2 * nd - 1)
+            for k in (0, 1, 2, 3, 4):
+                cross(k).start()
+            bias_copy.start()
+
+        p = mp * own + i
+        at = mult(p * slot, slot)
+        x = tok[pl.ds(at, slot), :]
+        made = nn(x, wq[...])
+        query = ((made[:, :half] + bias_q).astype(BF).astype(F32) * 0.125).astype(BF)
+        keyed = made[:, half : 2 * half].astype(BF)
+        value = (made[:, 2 * half :] + bias_v).astype(BF)
+        keyb[pl.ds(at, slot), :] = keyed
+        valb[pl.ds(at, slot), :] = value
+        bias = key_bias(p)
+        ctx[pl.ds(mult(i * slot, slot), slot), pl.ds(m_col, half)] = mix(query, keyed, value, bias)
+        first_row(p, x, query[0:16, :], keyed, value, bias)
         return carry
 
-    lax.fori_loop(0, count, attend, 0)
+    def attend_far(i, carry):
+        move_on(i, far_plan)
+        p = mp * own + i
+        x = tok[pl.ds(mult(p * slot, slot), slot), :]
+        made = nn(x, wq_far[...])
+        bias_far = bin_far[6:8, 0:half]
+        query = ((made[:, :half] + bias_far[0:1, :]).astype(BF).astype(F32) * 0.125).astype(BF)
+        keyed = made[:, half : 2 * half].astype(BF)
+        value = (made[:, 2 * half :] + bias_far[1:2, :]).astype(BF)
+        ctx[pl.ds(mult(i * slot, slot), slot), pl.ds(f_col, half)] = mix(
+            query, keyed, value, key_bias(p)
+        )
+        return carry
+
+    lax.fori_loop(0, own, attend_own, 0)
+    lax.fori_loop(0, own, attend_theirs, 0)
+
+    advance(*gap_plan)
+    bias_copy.wait_recv()
+    for k in range(3):
+        complete(k)
+    for k in range(5, chunks):
+        cross(k).start()
 
     pack[0:8, :] = stage[...]
     pack[8:16, :] = tcls[:, pl.ds(m_col, half)]
@@ -431,38 +483,23 @@
     pack[16 : 16 + q_rows, :] = queries[:, pl.ds(m_col, half)].astype(F32)
     gath[chip, core, mp] = pack[...].astype(BF)
 
-    def gather_copy(i, mine):
-        me = chip * 2 + mp
-        there = lax.rem(me + i, 2 * chips)
-        t_chip, t_mp = lax.div(there, 2), lax.rem(there, 2)
-        holder = gath.at[chip, core, mp] if mine else gath.at[t_chip, core, t_mp]
-        return remote(
-            gath.at[chip, core, mp],
-            holder,
-            g_send.at[i],
-            g_recv.at[me if mine else there],
-            (t_chip * 2 + core, t_mp),
-        )
-
     def gather_start(i, carry):
-        gather_copy(i, True).start()
+        there = lax.rem(chip * 2 + mp + i, 2 * chips)
+        here = gath.at[chip, core, mp]
+        remote(
+            here, here, g_send, g_recv, (lax.div(there, 2) * 2 + core, lax.rem(there, 2))
+        ).start()
         return carry
 
-    def gather_wait(i, carry):
-        gather_copy(i, False).wait_recv()
-        return carry
-
-    def gather_sent(i, carry):
-        gather_copy(i, True).wait_send()
-        return carry
+    gather_window = tok.at[pl.ds(0, (2 * chips - 1) * 16), :]
 
     lax.fori_loop(1, 2 * chips, gather_start, 0)
+
+    lax.fori_loop(0, own, attend_far, 0)
 
     for copy in loads[4:]:
         copy.wait()
-    tick(2)
-    tick(3)
-    complete(0)
+    complete(3)
     bo = row_of(b_out[...])
     g1 = row_of(gain_one[...])
     s1 = row_of(shift_one[...])
@@ -470,7 +507,7 @@
     bb = row_of(b_back[...])
 
     def feed_own(i, carry):
-        ctx_came(i).wait_recv()
+        move_on(i, feed_plan)
         at = mult(i * slot, slot)
         here = pl.ds(at, slot)
         x = tok[pl.ds(mult(mp * own_rows + i * slot, slot), slot), :].astype(F32)
@@ -481,50 +518,34 @@
         norm_low[here, :] = low
         total = norm + bb
         for u in range(blocks):
+            if u == 1:
+                move_on(i, feed_mid_plan)
             inner = nn(low, wi[mp, u]) + bin_own[u : u + 1, :]
             total = total + nn(gelu(inner).astype(BF), wb[mp, u])
         acc[here, :] = total
 
-        for j in range(own):
-
-            @pl.when(i == j)
-            def _():
-                if j + 4 < chunks + 2:
-                    tick(j + 4)
-
         return carry
 
     lax.fori_loop(0, own, feed_own, 0)
-    for i in range(own + 4, chunks + 2):
-        tick(i)
-
-    lax.fori_loop(1, 2 * chips, gather_wait, 0)
+
+    spent(gather_window, g_recv)
     to_sibling = remote(gath.at[:, core], gath.at[:, core], gs_send, gs_recv, sibling)
     to_sibling.start()
 
-    bias_copy.wait_recv()
     for u in range(blocks):
-        complete(1 + u)
+        complete(first_in + u)
 
         def feed_far_in(i, carry, u=u):
-            here = pl.ds(mult(i * slot, slot), slot)
+            move_on(i, in_plan[u])
+            here = pl.ds(mult(i * 2 * slot, slot), 2 * slot)
             inner = nn(norm_low[here, :], wi[far, u]) + bin_far[u : u + 1, :]
             act_far[u, here, :] = gelu(inner).astype(BF)
             return carry
 
-        lax.fori_loop(0, own, feed_far_in, 0)
-
-    for u in range(blocks - 1):
-        complete(1 + blocks + u)
-
-        def feed_far_back(i, carry, u=u):
-            here = pl.ds(mult(i * slot, slot), slot)
-            acc[here, :] += nn(act_far[u, here, :], wb[far, u])
-            return carry
-
-        lax.fori_loop(0, own, feed_far_back, 0)
-
-    complete(chunks - 1)
+        lax.fori_loop(0, own // 2, feed_far_in, 0)
+
+    for u in range(blocks):
+        complete(first_back + u)
 
     def out_copy(i, mine):
         side = mp if mine else far
@@ -541,7 +562,9 @@
 
     def finish(i, carry):
         here = pl.ds(mult(i * slot, slot), slot)
-        total = acc[here, :] + nn(act_far[blocks - 1, here, :], wb[far, blocks - 1])
+        total = acc[here, :]
+        for u in range(blocks):
+            total = total + nn(act_far[u, here, :], wb[far, u])
         scaled, _ = standard(total)
         acc[here, :] = scaled * g2
         obuf[0, here, :] = acc[here, pl.ds(m_col, half)].astype(BF)
@@ -642,66 +665,78 @@
     o_context[...] = ctx_all[:, pl.ds(m_col, half)]
     o_sums[5:6, 0:half] = jnp.sum(dc_all[...], axis=0, keepdims=True)
 
+    def stored(src, dst, k):
+        return pltpu.make_async_copy(src, dst, out_sem.at[k])
+
+    early = [
+        stored(src, dst, k)
+        for k, (src, dst) in enumerate(
+            (
+                (o_active, h_active),
+                (o_inner, h_inner),
+                (o_context, h_context),
+                (o_qcls, h_qcls),
+                (o_dctx, h_dctx),
+                (o_norm, h_norm),
+                (o_ffn, h_ffn),
+                (o_attn, h_attn),
+                (o_tok, h_tok),
+                (o_sums, h_sums),
+                (o_sums_in, h_sums_in),
+                (o_loss, h_loss),
+                (o_qgrad, h_qgrad),
+            )
+        )
+    ]
+    for copy in early:
+        copy.start()
+
     base = mult(dp * count, 8)
     fkind = count * 8
 
-    def attend_back(p, carry):
-        at = mult(p * slot, slot)
+    mark = jnp.logical_or(row_place == heads, row_place == heads + 1)
+    for p in range(count):
         d_row = dc_all[pl.ds(base + p, 1), :]
         q_row = qc_all[pl.ds(base + p, 1), :]
-        d_heads = jnp.where(head_mask, d_row, 0.0)
-        q_heads = jnp.where(head_mask, q_row, 0.0)
-        c = chance[p]
-        d_chance = nt(d_heads.astype(BF), valb[pl.ds(at, slot), :])
-        d_scores = c * (d_chance - jnp.sum(c * d_chance, axis=1, keepdims=True))
-        s_low = d_scores.astype(BF)
-        mark = jnp.logical_or(row_place == heads, row_place == heads + 1)
-        coef_own[pl.ds(mult(p * 16 + 8, 8), 8), :] = jnp.where(mark, first_key, d_scores)
-        factor[pl.ds(mult(fkind + p * 8, 8), 8), :] = nn(s_low, tok[pl.ds(at, slot), :])
-        spread = nn(s_low, keyb[pl.ds(at, slot), :])
-        dq_rows[pl.ds(p, 1), :] = 0.125 * jnp.sum(
-            jnp.where(head_mask, spread, 0.0), axis=0, keepdims=True
-        )
-        rank_f[pl.ds(mult(p * 16, 8), 8), 0:half] = d_heads
-        rank_f[pl.ds(mult(p * 16 + 8, 8), 8), 0:half] = q_heads
-        return carry
-
-    lax.fori_loop(0, count, attend_back, 0)
+        rank_f[p * 16 : p * 16 + 8, 0:half] = jnp.where(head_mask, d_row, 0.0)
+        rank_f[p * 16 + 8 : p * 16 + 16, 0:half] = jnp.where(head_mask, q_row, 0.0)
+    kept = rank_f[:, 0:half].astype(BF)
+    group = 4
+    for first in range(0, count, group):
+        d_scores = []
+        for p in range(first, first + group):
+            c = chance[p]
+            d_chance = nt(kept[p * 16 : p * 16 + 16, :], valb[p * slot : (p + 1) * slot, :])[0:8, :]
+            d_scores.append(c * (d_chance - jnp.sum(c * d_chance, axis=1, keepdims=True)))
+        for p, d in zip(range(first, first + group), d_scores):
+            s_low = d.astype(BF)
+            at = slice(p * slot, (p + 1) * slot)
+            coef_own[p * 16 + 8 : p * 16 + 16, :] = jnp.where(mark, first_key, d)
+            factor[fkind + p * 8 : fkind + p * 8 + 8, :] = nn(s_low, tok[at, :])
+            spread = nn(s_low, keyb[at, :])
+            dq_rows[p : p + 1, :] = 0.125 * jnp.sum(
+                jnp.where(head_mask, spread, 0.0), axis=0, keepdims=True
+            )
 
     turned = jnp.transpose(factor[...]).astype(BF)
-    fac_send[...] = turned
     dq = dq_rows[...]
     for b in range(half // 128):
         pack[b * 8 : b * 8 + 8, 0:128] = dq[:, b * 128 : b * 128 + 128]
     pack[half // 16 : 32, 0:128] = jnp.zeros((32 - half // 16, 128), F32)
-    dq_send[...] = pack[:, 0:128].astype(BF)
+    dq_low = pack[:, 0:128].astype(BF)
     share = width // nd
-    fac_all[dp] = fac_send[pl.ds(mult(dp * share, 16), share), :]
-    dq_all[dp] = dq_send[...]
-
-    def factor_copy(i, mine):
+    for j in range(nd):
+        fac_send[j, 0:share, :] = turned[j * share : (j + 1) * share, :]
+        fac_send[j, share:, :] = dq_low
+    o_factor[dp] = fac_send[dp]
+
+    def factor_start(i, carry):
         there = lax.rem(dp + i, nd)
-        holder = fac_all.at[dp] if mine else fac_all.at[there]
-        rows_out = fac_send.at[pl.ds(mult(there * share, 16), share), :]
-        return remote(
-            rows_out, holder, f_send.at[i], f_recv.at[dp if mine else there], (there, mp)
-        )
-
-    def dq_copy(i, mine):
-        there = lax.rem(dp + i, nd)
-        holder = dq_all.at[dp] if mine else dq_all.at[there]
-        return remote(
-            dq_send, holder, q_send.at[i], q_recv.at[dp if mine else there], (there, mp)
-        )
-
-    def factor_start(i, carry):
-        factor_copy(i, True).start()
-        dq_copy(i, True).start()
+        remote(fac_send.at[there], o_factor.at[dp], f_send, f_recv, (there, mp)).start()
         return carry
 
     lax.fori_loop(1, nd, factor_start, 0)
 
-    kept = rank_f[:, 0:half].astype(BF)
     even = lax.rem(lax.div(lax.broadcasted_iota(jnp.int32, (count * 16, 1), 0), 8), 2) == 0
     rank_v = nt(kept, wq[:, 2 * half :])
     rank_k = nt(kept, wq[:, half : 2 * half])
@@ -731,39 +766,30 @@
     o_coef[1] = coef_far[...]
     o_rank[1] = rank_far[...]
 
-    def factor_wait(i, carry):
-        factor_copy(i, False).wait_recv()
-        dq_copy(i, False).wait_recv()
-        return carry
-
-    lax.fori_loop(1, nd, factor_wait, 0)
-    o_factor[...] = fac_all[...]
-    o_dquery[...] = dq_all[...]
-
-    def factor_sent(i, carry):
-        factor_copy(i, True).wait_send()
-        dq_copy(i, True).wait_send()
-        return carry
-
-    lax.fori_loop(1, nd, factor_sent, 0)
+    factor_window = fac_send.at[pl.ds(0, nd - 1)]
+    spent(factor_window, f_recv)
+    last = [stored(o_factor, h_factor, 15), stored(o_coef, h_coef, 13), stored(o_rank, h_rank, 14)]
+    for copy in last:
+        copy.start()
+    spent(factor_window, f_send)
     coef_far_copy.wait_send()
     rank_copy.wait_send()
     bias_copy.wait_send()
-    lax.fori_loop(1, 2 * chips, gather_sent, 0)
+    spent(gather_window, g_send)
     to_sibling.wait_send()
     for k in range(chunks):
         cross(k).wait_send()
-        for n in range(8):
-            lane(k, n).wait_send()
+        spent(sent_bytes(k), w_send.at[k])
 
     def drain(i, carry):
-        ctx_copy(i).wait_send()
         out_copy(i, True).wait_send()
         out_copy(i, False).wait_recv()
         out_local(i).wait()
         return carry
 
     lax.fori_loop(0, own, drain, 0)
+    for copy in early + last:
+        copy.wait()
 
 
 def gradients(
@@ -772,7 +798,6 @@
     coef_in,
     rank_in,
     factor_in,
-    dquery_in,
     active_in,
     inner_in,
     context_in,
@@ -804,7 +829,6 @@
     coef,
     rank,
     factor,
-    dquery,
     active,
     inner,
     context,
@@ -833,7 +857,6 @@
         (coef_in, coef),
         (rank_in, rank),
         (factor_in, factor),
-        (dquery_in, dquery),
         (qcls_in, qcls),
         (dctx_in, dctx),
         (active_in, active),
@@ -896,8 +919,8 @@
     grad_k = jnp.zeros((share, half), F32)
     grad_v = jnp.zeros((share, half), F32)
     for s in range(0, nd, 4):
-        left_v = jnp.concatenate([factor[s + t][:, 0:fkind] for t in range(4)], axis=1)
-        left_k = jnp.concatenate([factor[s + t][:, fkind:] for t in range(4)], axis=1)
+        left_v = jnp.concatenate([factor[s + t, 0:share, :][:, 0:fkind] for t in range(4)], axis=1)
+        left_k = jnp.concatenate([factor[s + t, 0:share, :][:, fkind:] for t in range(4)], axis=1)
         grad_k = grad_k + nn(left_k, rhs[s * fkind : (s + 4) * fkind, 0:half])
         grad_v = grad_v + nn(left_v, rhs[s * fkind : (s + 4) * fkind, half:])
     grad_qkv[1] = grad_k
@@ -921,7 +944,7 @@
         grad_in[:, cols] = nn(norm_own, inner[u])
     dq_sum = []
     for b in range(half // 128):
-        cols = dquery[...].astype(F32)[:, b * 8 : b * 8 + 8, :].reshape(passages, 128)
+        cols = factor[:, share:, :].astype(F32)[:, b * 8 : b * 8 + 8, :].reshape(passages, 128)
         dq_sum.append(jnp.sum(cols, axis=0, keepdims=True))
         grad_qkv[0, :, b * 128 : b * 128 + 128] = nn(tok_own, cols.astype(BF))
 
@@ -980,7 +1003,7 @@
     units = w_in.shape[1]
     unit = 512
     blocks = units // unit
-    chunks = 1 + 2 * blocks
+    chunks = 4 + 2 * blocks
     own_rows = rows // 2
     passages = nd * count
     chips = nd // 2
@@ -994,27 +1017,27 @@
     shape = jax.ShapeDtypeStruct
     outs = [
         (shape((rows, half), BF), hbm),
-        (shape((2, count * 16, slot), BF), vmem),
-        (shape((2, count * 16, half), BF), vmem),
-        (shape((nd, share, 128), BF), vmem),
-        (shape((nd, 32, 128), BF), vmem),
-        (shape((blocks, passages, unit), BF), vmem),
-        (shape((blocks, passages, unit), BF), vmem),
-        (shape((passages, half), BF), vmem),
-        (shape((passages, half), BF), vmem),
-        (shape((passages, half), BF), vmem),
-        (shape((passages, width), BF), vmem),
-        (shape((passages, width), BF), vmem),
-        (shape((passages, width), BF), vmem),
-        (shape((passages, width), BF), vmem),
-        (shape((8, width), F32), vmem),
-        (shape((8, unit), F32), vmem),
-        (shape((8, q_pad), F32), vmem),
-        (shape((16, width), F32), vmem),
+        (shape((2, count * 16, slot), BF), hbm),
+        (shape((2, count * 16, half), BF), hbm),
+        (shape((nd, share + 32, 128), BF), hbm),
+        (shape((blocks, passages, unit), BF), hbm),
+        (shape((blocks, passages, unit), BF), hbm),
+        (shape((passages, half), BF), hbm),
+        (shape((passages, half), BF), hbm),
+        (shape((passages, half), BF), hbm),
+        (shape((passages, width), BF), hbm),
+        (shape((passages, width), BF), hbm),
+        (shape((passages, width), BF), hbm),
+        (shape((passages, width), BF), hbm),
+        (shape((8, width), F32), hbm),
+        (shape((8, unit), F32), hbm),
+        (shape((8, q_pad), F32), hbm),
+        (shape((16, width), F32), hbm),
     ]
     dma = pltpu.SemaphoreType.DMA
     scratch = [
         pltpu.VMEM((rows, width), BF),
+        pltpu.VMEM((width, 3 * half), BF),
         pltpu.VMEM((width, 3 * half), BF),
         pltpu.VMEM((width, width), BF),
         pltpu.VMEM((2, blocks, width, unit), BF),
@@ -1022,7 +1045,6 @@
         pltpu.VMEM((rows, half), BF),
         pltpu.VMEM((rows, half), BF),
         pltpu.VMEM((own_rows, width), BF),
-        pltpu.VMEM((own_rows, half), BF),
         pltpu.VMEM((own_rows, width), BF),
         pltpu.VMEM((own_rows, width), F32),
         pltpu.VMEM((blocks, own_rows, unit), BF),
@@ -1051,35 +1073,29 @@
         pltpu.VMEM((count * 16, half), BF),
         pltpu.VMEM((count * 16, half), BF),
         pltpu.VMEM((count * 16, half), BF),
-        pltpu.VMEM((width, 128), BF),
-        pltpu.VMEM((nd, share, 128), BF),
-        pltpu.VMEM((32, 128), BF),
-        pltpu.VMEM((nd, 32, 128), BF),
+        pltpu.VMEM((nd, share + 32, 128), BF),
         dma((5 + 2 * blocks,)),
         dma((chunks,)),
         dma((chunks,)),
-        dma((chunks, 8)),
-        dma((chunks, 8)),
+        dma((chunks,)),
+        dma((chunks, 5)),
         dma((count // 2,)),
         dma((count // 2,)),
         dma((count // 2,)),
-        dma((count // 2,)),
-        dma((count // 2,)),
-        dma((2 * chips,)),
-        dma((2 * chips,)),
         dma,
         dma,
-        dma((nd,)),
-        dma((nd,)),
-        dma((nd,)),
-        dma((nd,)),
+        dma,
+        dma,
+        dma,
+        dma,
         dma((2,)),
         dma((2,)),
         dma,
         dma,
         pltpu.VMEM((8, unit), F32),
         pltpu.VMEM((8, unit), F32),
-    ]
+        dma((16,)),
+    ] + [pltpu.VMEM(o[0].shape, o[0].dtype) for o in outs[1:]]
     made = pl.pallas_call(
         functools.partial(tower, nd, nd * q_rows),
         out_shape=[o[0] for o in outs],

time: 91.6 us -> 85.8 us (0.937)
  Pallas kernels: 90.8 us -> 84.8 us
    pallas_call x1, Pallas kernels: 84.8 us -> 78.8 us  [per_device(): pl.pallas_call(functools.partial(tower, nd, nd * q_rows), out_shape=[o[0]...]
where the time goes in v3:
time: 85.8 us; the launch traced here: 85.6 us
  Pallas kernels  84.8 us (99%)
    pallas_call x1, Pallas kernels, per_device(): pl.pallas_call(functools.partial(tower, nd, nd * q_rows), out_shape=[o[0]...  78.8 us
    pallas_call x1, Pallas kernels, per_device(): pl.pallas_call(functools.partial(gradients, nd), out_shape=[o[0] for o in...  6.01 us

profile of v3, /device:TPU:0, one launch (start us, length us, event | category | flops | bytes accessed | tf_op | source)
XLA Modules:
  0.0 85.6 jit_solution(13117949198382415367)
XLA Ops:
  0.7 78.8 %tower.1 = (bf16[2048,384]{1,0:T(8,128)(2,1)}, bf16[2,128,256]{2,1,0:T(8,128)(2,1)}, bf16[2,128,384]{2,1,0:T(8,128)(2,1)}, bf16[16,80,128]{2,1,0:T(8,128)(2,1)},...) custom-call(s32[8]{0:T(128)} %lengths.1, ...), custom_call_target="tpu_custom_call" | custom-call | tf_op jit(solution)/shard_map/tower/pallas_call | solution.py:1099
  79.4 6.0 %gradients.1 = (bf16[2048,384]{1,0:T(8,128)(2,1)}, f32[12]{0:T(128)}, f32[2048,384]{1,0:T(8,128)}, f32[12,768]{1,0:T(8,128)}, f32[3,48,384]{2,1,0:T(8,128)}, /*i...) custom-call(bf16[2048,384]{1,0:T(8,128)(2,1)} %get-tuple-element.47., ...), custom_call_target="tpu_custom_call" | custom-call | tf_op jit(solution)/shard_map/gradients/pallas_call | solution.py:1143

commit v4 on v3

--- a/solution.py
+++ b/solution.py
@@ -143,9 +143,7 @@
     rank_f,
     coef_own,
     coef_far,
-    rank_own,
-    rank_send,
-    rank_far,
+    dq_far,
     fac_send,
     loc_sem,
     ysend,
@@ -395,15 +393,16 @@
         factor[pl.ds(mult(p * 8, 8), 8), :] = nn(c_low, x)
 
     theirs_plan = (((1, 0),), (), ((1, 1),), ())
-    gap_plan = ((1, 2), (2, 0), (2, 1), (2, 2), (3, 0), (3, 1), (1, 3), (3, 2))
-    far_plan = ((), ((1, 4),), (), ((1, 5),))
-    feed_plan = ((), ((2, 4), (1, 7)), ((2, 5), (1, 8)), ((3, 4),))
-    feed_mid_plan = (((1, 6),), (), ((2, 6),), ((2, 7),))
-    in_plan = (
-        (((3, 5),), ()),
-        (((2, 8), (1, 9)), ((3, 6),)),
-        (((3, 7),), ((3, 8),)),
-    )
+    gap_plan = (
+        (1, 2), (2, 0), (1, 4), (2, 1), (2, 2), (3, 0), (2, 4), (3, 1), (1, 3), (3, 2)
+    )
+    far_plan = ((), ((3, 4), (1, 5)), (), ((1, 6),))
+    feed_plan = (
+        ((), ((2, 5), (1, 8)), (), ()),
+        (((1, 7),), (), ((2, 7),), ()),
+        ((), ((2, 6),), ((3, 5),), ((2, 8),)),
+    )
+    in_plan = ((((3, 6), (1, 9)), ((3, 7),)), ((), ()), (((3, 8),), ()))
 
     def move_on(i, plan):
         for j, steps in enumerate(plan):
@@ -434,7 +433,7 @@
         @pl.when(i == 1)
         def _():
             pl.semaphore_wait(barrier, 2 * nd - 1)
-            for k in (0, 1, 2, 3, 4):
+            for k in (0, 1, 2, 4, 3, 5):
                 cross(k).start()
             bias_copy.start()
 
@@ -469,13 +468,6 @@
     lax.fori_loop(0, own, attend_own, 0)
     lax.fori_loop(0, own, attend_theirs, 0)
 
-    advance(*gap_plan)
-    bias_copy.wait_recv()
-    for k in range(3):
-        complete(k)
-    for k in range(5, chunks):
-        cross(k).start()
-
     pack[0:8, :] = stage[...]
     pack[8:16, :] = tcls[:, pl.ds(m_col, half)]
     pack[16:32, :] = jnp.zeros((16, half), F32)
@@ -483,17 +475,27 @@
     pack[16 : 16 + q_rows, :] = queries[:, pl.ds(m_col, half)].astype(F32)
     gath[chip, core, mp] = pack[...].astype(BF)
 
+    here = gath.at[chip, core, mp]
+    to_pair = remote(here, here, gs_send.at[0], gs_recv.at[0], pair)
+    to_pair.start()
+    advance(*gap_plan)
+    bias_copy.wait_recv()
+    for k in range(3):
+        complete(k)
+    remote(
+        here, gath.at[chip, core, far], gs_send.at[0], gs_recv.at[0], pair
+    ).wait_recv()
+
     def gather_start(i, carry):
-        there = lax.rem(chip * 2 + mp + i, 2 * chips)
-        here = gath.at[chip, core, mp]
-        remote(
-            here, here, g_send, g_recv, (lax.div(there, 2) * 2 + core, lax.rem(there, 2))
-        ).start()
+        both = gath.at[chip, core]
+        there = lax.rem(chip + i, chips) * 2 + core
+        remote(both, both, g_send, g_recv, (there, mp)).start()
         return carry
 
-    gather_window = tok.at[pl.ds(0, (2 * chips - 1) * 16), :]
-
-    lax.fori_loop(1, 2 * chips, gather_start, 0)
+    lax.fori_loop(1, chips, gather_start, 0)
+    gather_window = tok.at[pl.ds(0, (chips - 1) * 32), :]
+    for k in range(6, chunks):
+        cross(k).start()
 
     lax.fori_loop(0, own, attend_far, 0)
 
@@ -507,7 +509,7 @@
     bb = row_of(b_back[...])
 
     def feed_own(i, carry):
-        move_on(i, feed_plan)
+        move_on(i, feed_plan[0])
         at = mult(i * slot, slot)
         here = pl.ds(at, slot)
         x = tok[pl.ds(mult(mp * own_rows + i * slot, slot), slot), :].astype(F32)
@@ -518,8 +520,8 @@
         norm_low[here, :] = low
         total = norm + bb
         for u in range(blocks):
-            if u == 1:
-                move_on(i, feed_mid_plan)
+            if u > 0:
+                move_on(i, feed_plan[u])
             inner = nn(low, wi[mp, u]) + bin_own[u : u + 1, :]
             total = total + nn(gelu(inner).astype(BF), wb[mp, u])
         acc[here, :] = total
@@ -527,10 +529,6 @@
         return carry
 
     lax.fori_loop(0, own, feed_own, 0)
-
-    spent(gather_window, g_recv)
-    to_sibling = remote(gath.at[:, core], gath.at[:, core], gs_send, gs_recv, sibling)
-    to_sibling.start()
 
     for u in range(blocks):
         complete(first_in + u)
@@ -544,39 +542,25 @@
 
         lax.fori_loop(0, own // 2, feed_far_in, 0)
 
-    for u in range(blocks):
-        complete(first_back + u)
-
-    def out_copy(i, mine):
-        side = mp if mine else far
-        there = out_act.at[pl.ds(mult(side * own_rows + i * slot, 16), slot), :]
-        return remote(
-            obuf.at[1, pl.ds(mult(i * slot, 16), slot), :], there, o_send.at[i], o_recv.at[i], pair
-        )
-
-    def out_local(i):
-        there = out_act.at[pl.ds(mult(mp * own_rows + i * slot, 16), slot), :]
-        return pltpu.make_async_copy(
-            obuf.at[0, pl.ds(mult(i * slot, 16), slot), :], there, o_loc.at[i]
-        )
-
-    def finish(i, carry):
-        here = pl.ds(mult(i * slot, slot), slot)
-        total = acc[here, :]
-        for u in range(blocks):
-            total = total + nn(act_far[u, here, :], wb[far, u])
-        scaled, _ = standard(total)
-        acc[here, :] = scaled * g2
-        obuf[0, here, :] = acc[here, pl.ds(m_col, half)].astype(BF)
-        obuf[1, here, :] = acc[here, pl.ds(f_col, half)].astype(BF)
-        out_copy(i, True).start()
-        out_local(i).start()
-        return carry
-
-    lax.fori_loop(0, own, finish, 0)
+    spent(gather_window, g_recv)
+    to_sibling = remote(
+        gath.at[:, core], gath.at[:, core], gs_send.at[1], gs_recv.at[1], sibling
+    )
+    to_sibling.start()
+
+    def feed_far_back(u):
+        def feed(i, carry):
+            here = pl.ds(mult(i * 2 * slot, slot), 2 * slot)
+            acc[here, :] += nn(act_far[u, here, :], wb[far, u])
+            return carry
+
+        lax.fori_loop(0, own // 2, feed, 0)
+
+    complete(first_back)
+    feed_far_back(0)
 
     remote(
-        gath.at[:, 1 - core], gath.at[:, 1 - core], gs_send, gs_recv, sibling
+        gath.at[:, 1 - core], gath.at[:, 1 - core], gs_send.at[1], gs_recv.at[1], sibling
     ).wait_recv()
     q_pad = nd * 16
     for h in range(2):
@@ -585,7 +569,6 @@
         ctx_all[:, cols] = block[:, :, 0:8].reshape(passages, half).astype(BF)
         tok_all[:, cols] = block[:, :, 8:16].reshape(passages, half).astype(BF)
         q_all[:, cols] = block[:, :, 16:32].reshape(q_pad, half).astype(BF)
-
     resid = tok_all[...].astype(F32) + nn(ctx_all[...], wo[...]) + bo
     scaled, inverse1 = standard(resid)
     xh1_all[...] = scaled
@@ -593,14 +576,51 @@
     low = norm.astype(BF)
     norm_all[...] = low
     total = norm + bb
-    for h in range(2):
+    for which, bias in ((mp, bin_own), (far, bin_far)):
         for u in range(blocks):
-            bias = jnp.where(mp == h, bin_own[u : u + 1, :], bin_far[u : u + 1, :])
-            inner = nn(low, wi[h, u]) + bias
-            inner_all[h, u] = inner
+            inner = nn(low, wi[which, u]) + bias[u : u + 1, :]
+            inner_all[which, u] = inner
             active = gelu(inner).astype(BF)
-            act_all[h, u] = active
-            total = total + nn(active, wb[h, u])
+            act_all[which, u] = active
+    for u in range(blocks):
+        total = total + nn(act_all[mp, u], wb[mp, u])
+    total = total + nn(act_all[far, 0], wb[far, 0])
+    for u in range(1, blocks - 1):
+        complete(first_back + u)
+        feed_far_back(u)
+        total = total + nn(act_all[far, u], wb[far, u])
+    complete(chunks - 1)
+
+    def out_copy(i, mine):
+        side = mp if mine else far
+        there = out_act.at[pl.ds(mult(side * own_rows + i * slot, 16), slot), :]
+        return remote(
+            obuf.at[1, pl.ds(mult(i * slot, 16), slot), :], there, o_send.at[i], o_recv.at[i], pair
+        )
+
+    def out_local(i):
+        there = out_act.at[pl.ds(mult(mp * own_rows + i * slot, 16), slot), :]
+        return pltpu.make_async_copy(
+            obuf.at[0, pl.ds(mult(i * slot, 16), slot), :], there, o_loc.at[i]
+        )
+
+    def finish(i, carry):
+        here = pl.ds(mult(i * slot, slot), slot)
+        total = acc[here, :] + nn(act_far[blocks - 1, here, :], wb[far, blocks - 1])
+        scaled, _ = standard(total)
+        acc[here, :] = scaled * g2
+        obuf[0, here, :] = acc[here, pl.ds(m_col, half)].astype(BF)
+        obuf[1, here, :] = acc[here, pl.ds(f_col, half)].astype(BF)
+        @pl.when(i < own - 1)
+        def _():
+            out_copy(i, True).start()
+
+        out_local(i).start()
+        return carry
+
+    lax.fori_loop(0, own, finish, 0)
+
+    total = total + nn(act_all[far, blocks - 1], wb[far, blocks - 1])
     xh2, inverse2 = standard(total)
     cls = (xh2 * g2).astype(BF)
     similar = nt(cls, q_all[...])
@@ -737,35 +757,52 @@
 
     lax.fori_loop(1, nd, factor_start, 0)
 
-    even = lax.rem(lax.div(lax.broadcasted_iota(jnp.int32, (count * 16, 1), 0), 8), 2) == 0
-    rank_v = nt(kept, wq[:, 2 * half :])
-    rank_k = nt(kept, wq[:, half : 2 * half])
-    rank_f[...] = jnp.where(even, rank_v, rank_k)
-    back_q = nt(dq.astype(BF), wq[:, 0:half])
-    for p in range(count):
-        rank_f[p * 16 + heads : p * 16 + heads + 1, :] = back_q[p : p + 1, :]
-        rank_f[p * 16 + heads + 1 : p * 16 + 8, :] = jnp.zeros((7 - heads, width), F32)
-        rank_f[p * 16 + 8 + heads : p * 16 + 16, :] = jnp.zeros((8 - heads, width), F32)
-    rank_send[...] = rank_f[:, pl.ds(f_col, half)].astype(BF)
     coef_low = coef_own[...].astype(BF)
     o_coef[0] = coef_low
     coef_far_copy = remote(o_coef.at[0], coef_far, m_send.at[0], m_recv.at[0], pair)
     coef_far_copy.start()
-    rank_copy = remote(rank_send, rank_far, m_send.at[1], m_recv.at[1], pair)
-    rank_copy.start()
-    d1_rows = d1_all[pl.ds(base, count), pl.ds(m_col, half)]
-    d1_high = d1_rows.astype(BF).astype(F32)
-    d1_low = d1_rows - d1_high
+    dq_copy = remote(dq_rows, dq_far, m_send.at[1], m_recv.at[1], pair)
+    dq_copy.start()
+    out_copy(own - 1, True).start()
+    kind = lax.rem(lax.div(lax.broadcasted_iota(jnp.int32, (count * 16, 1), 0), 8), 2)
+    d1_rows = d1_all[pl.ds(base, count), :]
+    d_far = nt(d1_rows.astype(BF), wo[pl.ds(mult(far * half, 128), half), :])
+    q_far = (nn(tcls[...].astype(BF), wq_far[:, 0:half]) + bin_far[6:7, 0:half]) * 0.125
     for p in range(count):
-        rank_f[p * 16 + 8 + heads : p * 16 + 9 + heads, pl.ds(m_col, half)] = d1_high[p : p + 1]
-        rank_f[p * 16 + 9 + heads : p * 16 + 10 + heads, pl.ds(m_col, half)] = d1_low[p : p + 1]
-    o_rank[0] = rank_f[:, pl.ds(m_col, half)].astype(BF)
-
+        rank_f[p * 16 : p * 16 + 8, 0:half] = jnp.where(head_mask, d_far[p : p + 1, :], 0.0)
+        rank_f[p * 16 + 8 : p * 16 + 16, 0:half] = jnp.where(head_mask, q_far[p : p + 1, :], 0.0)
+    kept_far = rank_f[:, 0:half].astype(BF)
+    my_rows = pl.ds(mult(mp * half, 128), half)
+
+    def rank_rows(left, right):
+        by_v = nt(left, right[my_rows, 2 * half :])
+        by_k = nt(left, right[my_rows, half : 2 * half])
+        return jnp.where(kind == 0, by_v, by_k)
+
+    rank_f[:, 0:half] = rank_rows(kept, wq)
+    rank_f[:, half:] = rank_rows(kept_far, wq_far)
+    d1_mine = d1_all[pl.ds(base, count), pl.ds(m_col, half)]
+    d1_high = d1_mine.astype(BF).astype(F32)
+    d1_low = d1_mine - d1_high
+
+    def first_rank(cols, back_q, high, low):
+        for p in range(count):
+            rank_f[p * 16 + heads : p * 16 + heads + 1, cols] = back_q[p : p + 1, :]
+            rank_f[p * 16 + heads + 1 : p * 16 + 8, cols] = jnp.zeros((7 - heads, half), F32)
+            rank_f[p * 16 + 8 + heads : p * 16 + 9 + heads, cols] = high[p : p + 1]
+            rank_f[p * 16 + 9 + heads : p * 16 + 10 + heads, cols] = low[p : p + 1]
+
+    mine = slice(0, half)
+    theirs = slice(half, width)
+    first_rank(mine, nt(dq.astype(BF), wq[my_rows, 0:half]), d1_high, d1_low)
+    o_rank[0] = rank_f[:, mine].astype(BF)
+
+    dq_copy.wait_recv()
+    nothing = jnp.zeros((count, half), F32)
+    first_rank(theirs, nt(dq_far[...].astype(BF), wq_far[my_rows, 0:half]), nothing, nothing)
+    o_rank[1] = rank_f[:, theirs].astype(BF)
     coef_far_copy.wait_recv()
-    rank_copy.wait_recv()
     o_coef[1] = coef_far[...]
-    o_rank[1] = rank_far[...]
-
     factor_window = fac_send.at[pl.ds(0, nd - 1)]
     spent(factor_window, f_recv)
     last = [stored(o_factor, h_factor, 15), stored(o_coef, h_coef, 13), stored(o_rank, h_rank, 14)]
@@ -773,10 +810,11 @@
         copy.start()
     spent(factor_window, f_send)
     coef_far_copy.wait_send()
-    rank_copy.wait_send()
+    dq_copy.wait_send()
     bias_copy.wait_send()
     spent(gather_window, g_send)
     to_sibling.wait_send()
+    to_pair.wait_send()
     for k in range(chunks):
         cross(k).wait_send()
         spent(sent_bytes(k), w_send.at[k])
@@ -1070,9 +1108,7 @@
         pltpu.VMEM((count * 16, width), F32),
         pltpu.VMEM((count * 16, slot), F32),
         pltpu.VMEM((count * 16, slot), BF),
-        pltpu.VMEM((count * 16, half), BF),
-        pltpu.VMEM((count * 16, half), BF),
-        pltpu.VMEM((count * 16, half), BF),
+        pltpu.VMEM((count, half), F32),
         pltpu.VMEM((nd, share + 32, 128), BF),
         dma((5 + 2 * blocks,)),
         dma((chunks,)),
@@ -1084,8 +1120,8 @@
         dma((count // 2,)),
         dma,
         dma,
-        dma,
-        dma,
+        dma((2,)),
+        dma((2,)),
         dma,
         dma,
         dma((2,)),

time: 85.8 us -> 84.4 us (0.984)
  Pallas kernels: 84.8 us -> 83.4 us
    pallas_call x1, Pallas kernels: 78.8 us -> 77.5 us  [per_device(): pl.pallas_call(functools.partial(tower, nd, nd * q_rows), out_shape=[o[0]...]
where the time goes in v4:
time: 84.4 us; the launch traced here: 84.3 us
  Pallas kernels  83.4 us (99%)
    pallas_call x1, Pallas kernels, per_device(): pl.pallas_call(functools.partial(tower, nd, nd * q_rows), out_shape=[o[0]...  77.5 us
    pallas_call x1, Pallas kernels, per_device(): pl.pallas_call(functools.partial(gradients, nd), out_shape=[o[0] for o in...  5.98 us

profile of v4, /device:TPU:0, one launch (start us, length us, event | category | flops | bytes accessed | tf_op | source)
XLA Modules:
  0.0 84.3 jit_solution(17982868129600456805)
XLA Ops:
  0.7 77.5 %tower.1 = (bf16[2048,384]{1,0:T(8,128)(2,1)}, bf16[2,128,256]{2,1,0:T(8,128)(2,1)}, bf16[2,128,384]{2,1,0:T(8,128)(2,1)}, bf16[16,80,128]{2,1,0:T(8,128)(2,1)},...) custom-call(s32[8]{0:T(128)} %lengths.1, ...), custom_call_target="tpu_custom_call" | custom-call | tf_op jit(solution)/shard_map/tower/pallas_call | solution.py:1135
  78.1 6.0 %gradients.1 = (bf16[2048,384]{1,0:T(8,128)(2,1)}, f32[12]{0:T(128)}, f32[2048,384]{1,0:T(8,128)}, f32[12,768]{1,0:T(8,128)}, f32[3,48,384]{2,1,0:T(8,128)}, /*i...) custom-call(bf16[2048,384]{1,0:T(8,128)(2,1)} %get-tuple-element.47., ...), custom_call_target="tpu_custom_call" | custom-call | tf_op jit(solution)/shard_map/gradients/pallas_call | solution.py:1179

commit v5 on v4

--- a/solution.py
+++ b/solution.py
@@ -241,49 +241,43 @@
     for copy in loads:
         copy.start()
 
-    first_in = 4
-    first_back = 4 + blocks
-    chunks = 4 + 2 * blocks
-    direct = (3, chunks - 1)
+    chunks = 7
+    direct = (3, 6)
+    lead = pl.ds(0, blocks - 1)
 
     def piece(k, q, c, which, side=None):
-        if k < 3 or first_in <= k < first_back:
-            size = width // 8
-            at = (c * 4 if q is None else c * 4 + q) * size
-            size = 4 * size if q is None else size
-            if side is not None:
-                size = size // 2
-                at = at + side * size
-            here = pl.ds(mult(at, 16), size)
-            return wq_far.at[here, pl.ds(k * half, half)] if k < 3 else wi.at[which, k - 4, here, :]
         cols = pl.ds(0, width) if side is None else pl.ds(side * half, half)
-        if k == 3:
-            size = half // 2
-            return wo.at[pl.ds(mult(which * half + c * size, 16), size), cols]
-        whole = k in direct or q is None
-        size = unit // 2 if whole else unit // 8
-        at = c * size if whole else (c * 4 + q) * size
-        return wb.at[which, k - first_back, pl.ds(mult(at, 16), size), cols]
+        if k in direct:
+            size = half // 2 if k == 3 else unit // 2
+            if k == 3:
+                return wo.at[pl.ds(mult(which * half + c * size, 16), size), cols]
+            return wb.at[which, blocks - 1, pl.ds(mult(c * size, 16), size), cols]
+        size = unit // 8 if k == 5 else width // 8
+        at = (c * 4 if q is None else c * 4 + q) * size
+        size = 4 * size if q is None else size
+        if k == 5:
+            return wb.at[which, lead, pl.ds(mult(at, 16), size), cols]
+        if side is not None:
+            size = size // 2
+            at = at + side * size
+        here = pl.ds(mult(at, 16), size)
+        return wq_far.at[here, pl.ds(k * half, half)] if k < 3 else wi.at[which, :, here, :]
 
     def sent_bytes(k):
+        if k in direct:
+            return piece(k, None, core, far)
         if k < 3:
             return wq_far.at[pl.ds(0, 7 * width // 8), pl.ds(k * half, half)]
-        if k == 3:
-            return piece(k, None, core, far)
-        if k < first_back:
-            return wi.at[far, k - 4, pl.ds(0, 7 * width // 8), :]
-        return wb.at[far, k - first_back, pl.ds(0, unit // 2 if k in direct else 7 * unit // 8), :]
+        if k == 4:
+            return wi.at[far, :, pl.ds(0, 7 * width // 8), :]
+        return wb.at[far, lead, pl.ds(0, 7 * unit // 8), :]
 
     def source(k):
-        if k < 3 or first_in <= k < first_back:
-            size = width // 8
-            here = pl.ds(mult((core * 4 + quarter) * size, 16), size)
-            return w_qkv.at[k, here, :] if k < 3 else w_in.at[here, pl.ds((k - 4) * unit, unit)]
+        if k < 3:
+            return w_qkv.at[k, pl.ds(mult((core * 4 + quarter) * (width // 8), 16), width // 8), :]
         if k == 3:
             return w_out.at[pl.ds(mult(core * (half // 2), 16), half // 2), :]
-        size = unit // 2 if k in direct else unit // 8
-        at = core * size if k in direct else (core * 4 + quarter) * size
-        return w_back.at[pl.ds(mult((k - first_back) * unit + at, 16), size), :]
+        return piece(k, quarter, core, mp)
 
     def remote(src, dst, ss, rs, device):
         return pltpu.make_async_remote_copy(
@@ -393,16 +387,10 @@
         factor[pl.ds(mult(p * 8, 8), 8), :] = nn(c_low, x)
 
     theirs_plan = (((1, 0),), (), ((1, 1),), ())
-    gap_plan = (
-        (1, 2), (2, 0), (1, 4), (2, 1), (2, 2), (3, 0), (2, 4), (3, 1), (1, 3), (3, 2)
-    )
-    far_plan = ((), ((3, 4), (1, 5)), (), ((1, 6),))
-    feed_plan = (
-        ((), ((2, 5), (1, 8)), (), ()),
-        (((1, 7),), (), ((2, 7),), ()),
-        ((), ((2, 6),), ((3, 5),), ((2, 8),)),
-    )
-    in_plan = ((((3, 6), (1, 9)), ((3, 7),)), ((), ()), (((3, 8),), ()))
+    gap_plan = ((2, 0), (1, 2), (2, 1), (3, 0), (2, 2), (1, 4), (3, 1), (3, 2))
+    far_plan = ((), (), (), ((1, 3),))
+    feed_plan = (((2, 4),), ((1, 5),), (), ((3, 4),))
+    in_plan = ((((2, 5), (1, 6)), ()), ((), ()), ((), ((3, 5),)))
 
     def move_on(i, plan):
         for j, steps in enumerate(plan):
@@ -433,7 +421,9 @@
         @pl.when(i == 1)
         def _():
             pl.semaphore_wait(barrier, 2 * nd - 1)
-            for k in (0, 1, 2, 4, 3, 5):
+            for copy in loads[4:]:
+                copy.wait()
+            for k in (0, 1, 2, 4, 3):
                 cross(k).start()
             bias_copy.start()
 
@@ -494,13 +484,11 @@
 
     lax.fori_loop(1, chips, gather_start, 0)
     gather_window = tok.at[pl.ds(0, (chips - 1) * 32), :]
-    for k in range(6, chunks):
+    for k in (5, 6):
         cross(k).start()
 
     lax.fori_loop(0, own, attend_far, 0)
 
-    for copy in loads[4:]:
-        copy.wait()
     complete(3)
     bo = row_of(b_out[...])
     g1 = row_of(gain_one[...])
@@ -509,7 +497,7 @@
     bb = row_of(b_back[...])
 
     def feed_own(i, carry):
-        move_on(i, feed_plan[0])
+        move_on(i, feed_plan)
         at = mult(i * slot, slot)
         here = pl.ds(at, slot)
         x = tok[pl.ds(mult(mp * own_rows + i * slot, slot), slot), :].astype(F32)
@@ -520,8 +508,6 @@
         norm_low[here, :] = low
         total = norm + bb
         for u in range(blocks):
-            if u > 0:
-                move_on(i, feed_plan[u])
             inner = nn(low, wi[mp, u]) + bin_own[u : u + 1, :]
             total = total + nn(gelu(inner).astype(BF), wb[mp, u])
         acc[here, :] = total
@@ -530,8 +516,8 @@
 
     lax.fori_loop(0, own, feed_own, 0)
 
+    complete(4)
     for u in range(blocks):
-        complete(first_in + u)
 
         def feed_far_in(i, carry, u=u):
             move_on(i, in_plan[u])
@@ -542,12 +528,6 @@
 
         lax.fori_loop(0, own // 2, feed_far_in, 0)
 
-    spent(gather_window, g_recv)
-    to_sibling = remote(
-        gath.at[:, core], gath.at[:, core], gs_send.at[1], gs_recv.at[1], sibling
-    )
-    to_sibling.start()
-
     def feed_far_back(u):
         def feed(i, carry):
             here = pl.ds(mult(i * 2 * slot, slot), 2 * slot)
@@ -556,8 +536,47 @@
 
         lax.fori_loop(0, own // 2, feed, 0)
 
-    complete(first_back)
+    complete(5)
     feed_far_back(0)
+
+    for u in range(1, blocks - 1):
+        feed_far_back(u)
+    spent(gather_window, g_recv)
+    to_sibling = remote(
+        gath.at[:, core], gath.at[:, core], gs_send.at[1], gs_recv.at[1], sibling
+    )
+    to_sibling.start()
+
+    complete(chunks - 1)
+
+    def out_copy(i, mine):
+        side = mp if mine else far
+        there = out_act.at[pl.ds(mult(side * own_rows + i * slot, 16), slot), :]
+        return remote(
+            obuf.at[1, pl.ds(mult(i * slot, 16), slot), :], there, o_send.at[i], o_recv.at[i], pair
+        )
+
+    def out_local(i):
+        there = out_act.at[pl.ds(mult(mp * own_rows + i * slot, 16), slot), :]
+        return pltpu.make_async_copy(
+            obuf.at[0, pl.ds(mult(i * slot, 16), slot), :], there, o_loc.at[i]
+        )
+
+    def finish(i, carry):
+        here = pl.ds(mult(i * slot, slot), slot)
+        total = acc[here, :] + nn(act_far[blocks - 1, here, :], wb[far, blocks - 1])
+        scaled, _ = standard(total)
+        acc[here, :] = scaled * g2
+        obuf[0, here, :] = acc[here, pl.ds(m_col, half)].astype(BF)
+        obuf[1, here, :] = acc[here, pl.ds(f_col, half)].astype(BF)
+        @pl.when(i < own - 1)
+        def _():
+            out_copy(i, True).start()
+
+        out_local(i).start()
+        return carry
+
+    lax.fori_loop(0, own, finish, 0)
 
     remote(
         gath.at[:, 1 - core], gath.at[:, 1 - core], gs_send.at[1], gs_recv.at[1], sibling
@@ -585,42 +604,9 @@
     for u in range(blocks):
         total = total + nn(act_all[mp, u], wb[mp, u])
     total = total + nn(act_all[far, 0], wb[far, 0])
-    for u in range(1, blocks - 1):
-        complete(first_back + u)
-        feed_far_back(u)
+    for u in range(1, blocks):
         total = total + nn(act_all[far, u], wb[far, u])
-    complete(chunks - 1)
-
-    def out_copy(i, mine):
-        side = mp if mine else far
-        there = out_act.at[pl.ds(mult(side * own_rows + i * slot, 16), slot), :]
-        return remote(
-            obuf.at[1, pl.ds(mult(i * slot, 16), slot), :], there, o_send.at[i], o_recv.at[i], pair
-        )
-
-    def out_local(i):
-        there = out_act.at[pl.ds(mult(mp * own_rows + i * slot, 16), slot), :]
-        return pltpu.make_async_copy(
-            obuf.at[0, pl.ds(mult(i * slot, 16), slot), :], there, o_loc.at[i]
-        )
-
-    def finish(i, carry):
-        here = pl.ds(mult(i * slot, slot), slot)
-        total = acc[here, :] + nn(act_far[blocks - 1, here, :], wb[far, blocks - 1])
-        scaled, _ = standard(total)
-        acc[here, :] = scaled * g2
-        obuf[0, here, :] = acc[here, pl.ds(m_col, half)].astype(BF)
-        obuf[1, here, :] = acc[here, pl.ds(f_col, half)].astype(BF)
-        @pl.when(i < own - 1)
-        def _():
-            out_copy(i, True).start()
-
-        out_local(i).start()
-        return carry
-
-    lax.fori_loop(0, own, finish, 0)
-
-    total = total + nn(act_all[far, blocks - 1], wb[far, blocks - 1])
+
     xh2, inverse2 = standard(total)
     cls = (xh2 * g2).astype(BF)
     similar = nt(cls, q_all[...])
@@ -1041,7 +1027,7 @@
     units = w_in.shape[1]
     unit = 512
     blocks = units // unit
-    chunks = 4 + 2 * blocks
+    chunks = 7
     own_rows = rows // 2
     passages = nd * count
     chips = nd // 2

time: 84.4 us -> 82 us (0.972)
  Pallas kernels: 83.4 us -> 81 us
    pallas_call x1, Pallas kernels: 77.5 us -> 75 us  [per_device(): pl.pallas_call(functools.partial(tower, nd, nd * q_rows), out_shape=[o[0]...]
where the time goes in v5:
time: 82 us; the launch traced here: 81.8 us
  Pallas kernels  81 us (99%)
    pallas_call x1, Pallas kernels, per_device(): pl.pallas_call(functools.partial(tower, nd, nd * q_rows), out_shape=[o[0]...  75 us
    pallas_call x1, Pallas kernels, per_device(): pl.pallas_call(functools.partial(gradients, nd), out_shape=[o[0] for o in...  5.99 us

profile of v5, /device:TPU:0, one launch (start us, length us, event | category | flops | bytes accessed | tf_op | source)
XLA Modules:
  0.0 81.8 jit_solution(9056675801286865099)
XLA Ops:
  0.7 75.0 %tower.1 = (bf16[2048,384]{1,0:T(8,128)(2,1)}, bf16[2,128,256]{2,1,0:T(8,128)(2,1)}, bf16[2,128,384]{2,1,0:T(8,128)(2,1)}, bf16[16,80,128]{2,1,0:T(8,128)(2,1)},...) custom-call(s32[8]{0:T(128)} %lengths.1, ...), custom_call_target="tpu_custom_call" | custom-call | tf_op jit(solution)/shard_map/tower/pallas_call | solution.py:1121
  75.7 6.0 %gradients.1 = (bf16[2048,384]{1,0:T(8,128)(2,1)}, f32[12]{0:T(128)}, f32[2048,384]{1,0:T(8,128)}, f32[12,768]{1,0:T(8,128)}, f32[3,48,384]{2,1,0:T(8,128)}, /*i...) custom-call(bf16[2048,384]{1,0:T(8,128)(2,1)} %get-tuple-element.47., ...), custom_call_target="tpu_custom_call" | custom-call | tf_op jit(solution)/shard_map/gradients/pallas_call | solution.py:1165

commit v6 on v5

--- a/solution.py
+++ b/solution.py
@@ -423,9 +423,9 @@
             pl.semaphore_wait(barrier, 2 * nd - 1)
             for copy in loads[4:]:
                 copy.wait()
+            bias_copy.start()
             for k in (0, 1, 2, 4, 3):
                 cross(k).start()
-            bias_copy.start()
 
         p = mp * own + i
         at = mult(p * slot, slot)
@@ -472,9 +472,6 @@
     bias_copy.wait_recv()
     for k in range(3):
         complete(k)
-    remote(
-        here, gath.at[chip, core, far], gs_send.at[0], gs_recv.at[0], pair
-    ).wait_recv()
 
     def gather_start(i, carry):
         both = gath.at[chip, core]
@@ -482,12 +479,15 @@
         remote(both, both, g_send, g_recv, (there, mp)).start()
         return carry
 
-    lax.fori_loop(1, chips, gather_start, 0)
     gather_window = tok.at[pl.ds(0, (chips - 1) * 32), :]
     for k in (5, 6):
         cross(k).start()
 
     lax.fori_loop(0, own, attend_far, 0)
+    remote(
+        here, gath.at[chip, core, far], gs_send.at[0], gs_recv.at[0], pair
+    ).wait_recv()
+    lax.fori_loop(1, chips, gather_start, 0)
 
     complete(3)
     bo = row_of(b_out[...])

time: 82 us -> 83.6 us (1.020)
  Pallas kernels: 81 us -> 82.6 us
    pallas_call x1, Pallas kernels: 75 us -> 76.6 us  [per_device(): pl.pallas_call(functools.partial(tower, nd, nd * q_rows), out_shape=[o[0]...]
where the time goes in v6:
time: 83.6 us; the launch traced here: 83.4 us
  Pallas kernels  82.6 us (99%)
    pallas_call x1, Pallas kernels, per_device(): pl.pallas_call(functools.partial(tower, nd, nd * q_rows), out_shape=[o[0]...  76.6 us
    pallas_call x1, Pallas kernels, per_device(): pl.pallas_call(functools.partial(gradients, nd), out_shape=[o[0] for o in...  6.02 us

profile of v6, /device:TPU:0, one launch (start us, length us, event | category | flops | bytes accessed | tf_op | source)
XLA Modules:
  0.0 83.4 jit_solution(16067080466305735591)
XLA Ops:
  0.7 76.6 %tower.1 = (bf16[2048,384]{1,0:T(8,128)(2,1)}, bf16[2,128,256]{2,1,0:T(8,128)(2,1)}, bf16[2,128,384]{2,1,0:T(8,128)(2,1)}, bf16[16,80,128]{2,1,0:T(8,128)(2,1)},...) custom-call(s32[8]{0:T(128)} %lengths.1, ...), custom_call_target="tpu_custom_call" | custom-call | tf_op jit(solution)/shard_map/tower/pallas_call | solution.py:1121
  77.2 6.0 %gradients.1 = (bf16[2048,384]{1,0:T(8,128)(2,1)}, f32[12]{0:T(128)}, f32[2048,384]{1,0:T(8,128)}, f32[12,768]{1,0:T(8,128)}, f32[3,48,384]{2,1,0:T(8,128)}, /*i...) custom-call(bf16[2048,384]{1,0:T(8,128)(2,1)} %get-tuple-element.47., ...), custom_call_target="tpu_custom_call" | custom-call | tf_op jit(solution)/shard_map/gradients/pallas_call | solution.py:1165

commit v7 on v5

--- a/solution.py
+++ b/solution.py
@@ -541,12 +541,9 @@
 
     for u in range(1, blocks - 1):
         feed_far_back(u)
-    spent(gather_window, g_recv)
     to_sibling = remote(
         gath.at[:, core], gath.at[:, core], gs_send.at[1], gs_recv.at[1], sibling
     )
-    to_sibling.start()
-
     complete(chunks - 1)
 
     def out_copy(i, mine):
@@ -563,6 +560,11 @@
         )
 
     def finish(i, carry):
+        @pl.when(i == 1)
+        def _():
+            spent(gather_window, g_recv)
+            to_sibling.start()
+
         here = pl.ds(mult(i * slot, slot), slot)
         total = acc[here, :] + nn(act_far[blocks - 1, here, :], wb[far, blocks - 1])
         scaled, _ = standard(total)

time: 82 us -> 82 us (level)
  no operation moved by 1% of the time
where the time goes in v7:
time: 82 us; the launch traced here: 81.8 us
  Pallas kernels  81 us (99%)
    pallas_call x1, Pallas kernels, per_device(): pl.pallas_call(functools.partial(tower, nd, nd * q_rows), out_shape=[o[0]...  75 us
    pallas_call x1, Pallas kernels, per_device(): pl.pallas_call(functools.partial(gradients, nd), out_shape=[o[0] for o in...  6 us

profile of v7, /device:TPU:0, one launch (start us, length us, event | category | flops | bytes accessed | tf_op | source)
XLA Modules:
  0.0 81.8 jit_solution(16022611299560451170)
XLA Ops:
  0.7 75.0 %tower.1 = (bf16[2048,384]{1,0:T(8,128)(2,1)}, bf16[2,128,256]{2,1,0:T(8,128)(2,1)}, bf16[2,128,384]{2,1,0:T(8,128)(2,1)}, bf16[16,80,128]{2,1,0:T(8,128)(2,1)},...) custom-call(s32[8]{0:T(128)} %lengths.1, ...), custom_call_target="tpu_custom_call" | custom-call | tf_op jit(solution)/shard_map/tower/pallas_call | solution.py:1123
  75.7 6.0 %gradients.1 = (bf16[2048,384]{1,0:T(8,128)(2,1)}, f32[12]{0:T(128)}, f32[2048,384]{1,0:T(8,128)}, f32[12,768]{1,0:T(8,128)}, f32[3,48,384]{2,1,0:T(8,128)}, /*i...) custom-call(bf16[2048,384]{1,0:T(8,128)(2,1)} %get-tuple-element.47., ...), custom_call_target="tpu_custom_call" | custom-call | tf_op jit(solution)/shard_map/gradients/pallas_call | solution.py:1167
